TPU v7x, 512 devices: a whole 4x8x8 slice. The times are simulated.
512 devices in a mesh: sec: 4 (over z_hi), fsdp: 128 (over z_lo, y, x, core).
Axes of the slice: x: 4, y: 8, z: 8 (z_hi: 4, z_lo: 2; z = z_hi * 2 + z_lo), core: 2. Of those that a mesh axis runs over, the one named last changes fastest.
Arguments:
- hidden: bfloat16 [65536, 4096], P('fsdp', 'sec'), may hold values from -24 to 24
- window_proj: bfloat16 [4, 4096, 512], P('sec', 'fsdp'), may hold values from -0.09375 to 0.09375
- head_weights: bfloat16 [4, 512], P('sec'), may hold values from -0.25 to 0.25
- ref_logprob: float32 [128, 512], P('fsdp'), may hold values from -4 to 0
- resp_spans: int32 [128, 2], P('fsdp'), may hold values from 64 to 512, as said below
Outputs:
- actor_grad: float32 [4, 4096, 256], P('sec', 'fsdp')
- advantage: float32 [128, 512], P('fsdp')
Inputs may be any that keep to these rules, and one draw needn't show every extreme that they name: `resp_spans`: column 0 is a sequence's first response position, between 64 and 255; column 1 is one past its last response position, larger than column 0.
All inputs are finite; a program needn't handle non-finite values.
Results may differ from a plain program's by a relative error of at most 0.0085.
Values may be sent and summed in bfloat16 or wider, within the bound.
A program may use at most 64 MiB of HBM per device.

v0:
```python
import jax
import jax.numpy as jnp
from jax import lax
from jax.sharding import Mesh
from jax.sharding import PartitionSpec as P

FSDP = ("fsdp_0", "fsdp_1", "fsdp_2", "fsdp_3")


KL_COEF = 0.1
DISCOUNT = 1.0
TRACE_DECAY = 0.95
NORM_EPS = 1e-05


def copy_for_each(array, axis):
    copies = jnp.broadcast_to(array, (lax.axis_size(axis), *array.shape))
    return lax.all_to_all(copies, axis, split_axis=0, concat_axis=0, tiled=True)


def laid_out(tiles, dim):
    tiles = jnp.moveaxis(tiles, 0, dim)
    dims = tiles.shape
    return tiles.reshape(*dims[:dim], dims[dim] * dims[dim + 1], *dims[dim + 2 :])


def gathered_by_axis(array, axes, dim):
    far, near = axes
    tiles = copy_for_each(copy_for_each(array, far), near)
    return laid_out(tiles.swapaxes(0, 1).reshape(-1, *array.shape), dim)


def gathered_copies(array, axis, dim):
    tiles = copy_for_each(array, axis)
    return laid_out(tiles, dim)


def from_behind(array, axis, by):
    length = lax.axis_size(axis)
    pairs = [(i, i + by) for i in range(length) if 0 <= i + by < length]
    return lax.ppermute(array, axis, pairs)


def split_up(array, dim, length):
    dims = array.shape
    tiles = array.reshape(*dims[:dim], length, dims[dim] // length, *dims[dim + 1 :])
    return jnp.moveaxis(tiles, dim, 0)


def sent_and_summed(array, axis, dim):
    tiles = split_up(array, dim, lax.axis_size(axis))
    arrived = lax.all_to_all(tiles, axis, split_axis=0, concat_axis=0, tiled=True)
    return arrived.sum(axis=0)


def sum_by_axis(array, axes, dim):
    far, near = axes
    tiles = split_up(array, dim, lax.axis_size(far))
    nearer = sent_and_summed(tiles, near, dim + 1)
    arrived = lax.all_to_all(nearer, far, split_axis=0, concat_axis=0, tiled=True)
    return arrived.sum(axis=0)


def silu_slope(values):
    sigmoid = jax.nn.sigmoid(values)
    return sigmoid * (1.0 + values * (1.0 - sigmoid))


def normalize(hidden):
    widened = hidden.astype(jnp.float32)
    meansq = jnp.mean(widened * widened, axis=1, keepdims=True)
    return (widened * lax.rsqrt(meansq + NORM_EPS)).astype(jnp.bfloat16)


def advantage_of(log_prob, value_est, scores, ref_logprob, resp_spans, length):
    position = lax.broadcasted_iota(jnp.int32, (1, length), 1)
    starts = resp_spans[:, 0:1]
    ending = resp_spans[:, 1:2]
    inside = ((position >= starts) & (position < ending)).astype(jnp.float32)
    last_tok = (position == ending - 1).astype(jnp.float32)
    follow = (position + 1 < ending).astype(jnp.float32)
    reward = -KL_COEF * (log_prob - ref_logprob) * inside + scores * last_tok
    next_value = jnp.concatenate(
        [value_est[:, 1:], jnp.zeros((value_est.shape[0], 1), jnp.float32)], axis=1
    )
    deltas = (reward + DISCOUNT * next_value * follow - value_est) * inside
    source_pos = lax.broadcasted_iota(jnp.int32, (length, length), 0)
    target_pos = lax.broadcasted_iota(jnp.int32, (length, length), 1)
    spacing = source_pos - target_pos
    decays = jnp.where(
        spacing >= 0,
        jnp.power(jnp.float32(DISCOUNT * TRACE_DECAY), jnp.maximum(spacing, 0).astype(jnp.float32)),
        jnp.float32(0.0),
    )
    advantage = jnp.dot(deltas, decays, precision=lax.Precision.HIGHEST) * inside
    counts = (ending - starts).astype(jnp.float32)
    signal = -advantage / counts
    return (advantage, signal)


def shards(hidden, window_proj, head_weights, ref_logprob, resp_spans):
    features = lax.all_gather(hidden, "sec", axis=1, tiled=True)
    normed = normalize(features)
    weights = window_proj[0]
    own_head = head_weights[0]
    tok_rows = normed.shape[0]
    half_cols = own_head.shape[0] // 2
    whole_slab = gathered_by_axis(weights, (("fsdp_0", "fsdp_1", "fsdp_2"), "fsdp_3"), 0)
    pre_act = jnp.dot(normed, whole_slab, preferred_element_type=jnp.float32).astype(jnp.bfloat16)
    own_sum = jnp.sum(
        own_head.astype(jnp.float32) * jax.nn.silu(pre_act.astype(jnp.float32)),
        axis=1,
        keepdims=True,
    )
    totals = gathered_copies(own_sum, "sec", 1)
    shaped = ref_logprob.shape
    log_prob = (totals[:, 0] + totals[:, 1]).reshape(shaped)
    value_est = totals[:, 2].reshape(shaped)
    scores = totals[:, 3].reshape(shaped)
    advantage, signal = advantage_of(
        log_prob, value_est, scores, ref_logprob, resp_spans, shaped[1]
    )
    far_side = lax.axis_index("sec") >= 2
    moved_pre, moved_head = from_behind((pre_act[:, half_cols:], own_head[half_cols:]), "sec", 2)
    chosen_pre = jnp.where(far_side, moved_pre, pre_act[:, :half_cols])
    chosen_head = jnp.where(far_side, moved_head, own_head[:half_cols])
    flat_signal = signal.reshape(tok_rows)
    slopes = (
        flat_signal[:, None]
        * chosen_head.astype(jnp.float32)[None, :]
        * silu_slope(chosen_pre.astype(jnp.float32))
    ).astype(jnp.bfloat16)
    grad_part = sum_by_axis(
        lax.dot_general(
            normed, slopes, (((0,), (0,)), ((), ())), preferred_element_type=jnp.float32
        ),
        (("fsdp_0", "fsdp_1", "fsdp_2"), "fsdp_3"),
        0,
    )
    return (grad_part[None], advantage)


def solution(mesh):
    finer = Mesh(
        mesh.devices.reshape(mesh.shape["sec"], 2, 8, 4, 2),
        ("sec", "fsdp_0", "fsdp_1", "fsdp_2", "fsdp_3"),
    )
    return jax.shard_map(
        shards,
        mesh=finer,
        in_specs=(
            P(FSDP, "sec"),
            P("sec", FSDP, None),
            P("sec", None),
            P(FSDP, None),
            P(FSDP, None),
        ),
        out_specs=(P("sec", FSDP, None), P(FSDP, None)),
        check_vma=False,
    )
```

profile of v0, /device:TPU:1, one launch (start us, length us, event | category | flops | bytes accessed | tf_op | source)
XLA Modules:
  0.0 241.3 jit_solution(5176253014631633852)
XLA Ops:
  7.2 0.0 copy-start.1
  7.2 0.0 copy-start.2
  7.2 0.0 all-gather.2.cloned.1.call-start
  7.2 0.7 all-gather.2.cloned.1.call-update
  7.9 2.3 broadcast_in_dim.20
  10.3 12.9 %all-to-all-start = ((bf16[64,32,512]{2,1,0:T(8,128)(2,1)}), bf16[64,32,512]{2,1,0:T(8,128)(2,1)S(1)}, u32[]{:S(2)}, u32[]{:S(2)}) async-start(bf16[64,32,512]{2,1,0:T(8,128)(2,1)} %broadcast_in_dim.20), calls=%async_computation | async-start | bytes 4194304 | tf_op jit(solution)/shard_map/all_to_all | solution.py:18
  23.2 0.0 copy-done.1
  23.2 9.7 %collective-permute-start = (bf16[256]{0:T(256)(128)(2,1)S(1)}, bf16[256]{0:T(256)(128)(2,1)S(1)}, u32[]{:S(2)}, u32[]{:S(2)}) collective-permute-start(bf16[256]{0:T(256)(128)(2,1)S(1)} %get-tuple-element.3), channel_id=1, source_target_pairs={{0,256},{128,384},{1,257},{129,385},{2,258},{130,386},{3,259},{131... | collective-permute-start | bytes 1544 | tf_op jit(solution)/shard_map/ppermute | solution.py:41
  33.0 0.0 copy-done.2
  33.0 0.6 fusion.66
  35.4 35.6 %all-to-all-done = bf16[64,32,512]{2,1,0:T(8,128)(2,1)S(1)} async-done(((bf16[64,32,512]{2,1,0:T(8,128)(2,1)}), bf16[64,32,512]{2,1,0:T(8,128)(2,1)S(1)}, u32[]{:S(2)}, u32[]{:S(2)}) %all-to-all-start) | async-done | bytes 2097184 | tf_op jit(solution)/shard_map/all_to_all | solution.py:18
  71.0 0.7 broadcast_in_dim.21
  71.7 10.6 %all_to_all.25 = bf16[2,64,32,512]{3,2,1,0:T(8,128)(2,1)S(1)} all-to-all(bf16[2,64,32,512]{3,2,1,0:T(8,128)(2,1)S(1)} %broadcast_in_dim.21), channel_id=1, replica_groups=mesh['sec'=4,'fsdp_0'=2,'fsdp_1'=8,'fsdp_2'=4,'fsdp_3'=2] {'fsdp_3'}, dimensions={0} | all-to-all | bytes 8388608 | tf_op jit(solution)/shard_map/all_to_all | solution.py:18
  82.3 2.5 %copy.9 = bf16[2,64,32,512]{3,2,0,1:T(8,128)(2,1)} copy(bf16[2,64,32,512]{3,2,1,0:T(8,128)(2,1)S(1)} %all_to_all.25) | data formatting | bytes 8388608 | tf_op jit(solution)/shard_map/all_to_all | solution.py:18
  84.8 37.8 %all-gather.2.cloned.1.call-done = bf16[512,4096]{1,0:T(8,128)(2,1)} async-done(((bf16[512,1024]{1,0:T(8,128)(2,1)}), bf16[512,4096]{1,0:T(8,128)(2,1)}) %all-gather.2.cloned.1.call-update) | async-done | bytes 4194320 | tf_op jit(solution)/shard_map/all_gather | solution.py:102
  122.6 0.0 copy-start
  122.6 3.2 %fusion = f32[512]{0:T(512)S(1)} fusion(bf16[512,4096]{1,0:T(8,128)(2,1)} %all-gather.2.cloned.1.call-done), kind=kLoop, calls=%fused_computation.2 | loop fusion | flops 6290944 | bytes 4196352 | tf_op jit(solution)/shard_map/reduce_sum | solution.py:71
  125.8 0.2 copy-done
  126.0 0.0 copy-start.3
  126.0 4.9 %fusion.19 = (f32[512]{0:T(512)S(1)}, bf16[512,512]{0,1:T(8,128)(2,1)S(1)}) fusion(f32[512]{0:T(512)S(1)} %bitcast.52, bf16[4096,512]{1,0:T(8,128)(2,1)} %bitcast.45, bf16[512,4096]{1,0:T(8,128)(2,1)S(1)} %copy-done, f32[512]{0:T(512)S(1)} %add_rsqrt_fusion), kind=kOutput, calls=%fused_computation.21 | convolution fusion | flops 2155871744 | bytes 8919040 | tf_op jit(solution)/shard_map/dot_general | solution.py:109
  130.9 0.6 broadcast_in_dim.22
  131.6 5.5 %all-to-all-start.2 = ((f32[4,512,1]{1,2,0:T(1,128)}), f32[4,512,1]{1,2,0:T(1,128)S(1)}, u32[]{:S(2)}, u32[]{:S(2)}) async-start(f32[4,512,1]{1,2,0:T(1,128)} %broadcast_in_dim.22), calls=%async_computation.2 | async-start | bytes 16384 | tf_op jit(solution)/shard_map/all_to_all | solution.py:18
  137.0 0.0 collective-permute-done
  137.1 7.3 %collective-permute-start.1 = (bf16[512,256]{0,1:T(8,128)(2,1)S(1)}, bf16[512,256]{0,1:T(8,128)(2,1)S(1)}, u32[]{:S(2)}, u32[]{:S(2)}) collective-permute-start(bf16[512,256]{0,1:T(8,128)(2,1)S(1)} %slice.57), channel_id=1, source_target_pairs={{0,256},{128,384},{1,257},{129,385},{2,258},{130,386},{3,259},{131... | collective-permute-start | bytes 786440 | tf_op jit(solution)/shard_map/ppermute | solution.py:41
  144.4 0.0 all-to-all-done.2
  144.4 0.1 slice.56
  144.5 0.0 copy-done.3
  144.5 1.9 fusion.13
  146.4 1.8 negate_divide_fusion
  148.1 0.8 collective-permute-done.1
  148.9 4.1 %fusion.2 = f32[4096,256]{1,0:T(8,128)S(1)} fusion(bf16[512,4096]{1,0:T(8,128)(2,1)} %all-gather.2.cloned.1.call-done, f32[512]{0:T(512)S(1)} %add_rsqrt_fusion, bf16[512,256]{0,1:T(8,128)(2,1)S(1)} %collective-permute-done.1, bf16[512,512]{0,1:T(8,128)(2,1)S(1)} %get-tuple-element.9, f32[256]{0:T(256)S(1)} %fusion.57, f32[512]{0:T(512)S(1)} %get-tuple-element.4, ...), kind=kOutput, calls=%fused_computation.5 | convolution fusion | flops 1081606144 | bytes 8918017 | tf_op jit(solution)/shard_map/dot_general | solution.py:134
  153.1 0.6 copy.14
  153.6 9.7 %all_to_all.26 = f32[2,64,32,256]{3,2,1,0:T(8,128)} all-to-all(f32[2,64,32,256]{3,2,1,0:T(8,128)S(1)} %bitcast.44), channel_id=1, replica_groups=mesh['sec'=4,'fsdp_0'=2,'fsdp_1'=8,'fsdp_2'=4,'fsdp_3'=2] {'fsdp_3'}, dimensions={0} | all-to-all | bytes 8388608 | tf_op jit(solution)/shard_map/all_to_all | solution.py:52
  163.4 2.8 %reduce_sum.38 = f32[64,32,256]{2,1,0:T(8,128)S(1)} reduce(f32[2,64,32,256]{3,2,1,0:T(8,128)} %all_to_all.26, f32[]{:T(128)} %constant.13.clone.1), dimensions={0}, to_apply=%region_2.3 | reduce | flops 524288 | bytes 6291460 | tf_op jit(solution)/shard_map/reduce_sum | solution.py:53
  166.2 65.9 %all_to_all.27 = f32[64,32,256]{2,1,0:T(8,128)} all-to-all(f32[64,32,256]{2,1,0:T(8,128)S(1)} %reduce_sum.38), channel_id=1, replica_groups=mesh['sec'=4,'fsdp_0'=2,'fsdp_1'=8,'fsdp_2'=4,'fsdp_3'=2] {'fsdp_0','fsd..., dimensions={0} | all-to-all | bytes 4194304 | tf_op jit(solution)/shard_map/all_to_all | solution.py:60
  232.1 2.3 reduce_sum.39
  (7 shorter events, 0.1 us)
Async XLA Ops:
  7.2 16.0 %copy-start.1 = (bf16[1,512]{1,0:T(2,128)(2,1)S(1)}, bf16[1,512]{1,0:T(2,128)(2,1)}, u32[]{:S(2)}) copy-start(bf16[1,512]{1,0:T(2,128)(2,1)} %param.7) | copy-start | bytes 3076
  7.2 25.8 %copy-start.2 = (s32[1,2]{1,0:T(1,128)S(1)}, s32[1,2]{1,0:T(1,128)}, u32[]{:S(2)}) copy-start(s32[1,2]{1,0:T(1,128)} %param.9) | copy-start | bytes 28
  7.2 115.4 %all-gather.2.cloned.1.call-start = ((), (), s32[]{:S(2)}) async-start(), calls=%async_computation.5 | async-start | bytes 5242880 | tf_op jit(solution)/shard_map/all_gather | solution.py:102
  10.3 60.8 %all-to-all-start = ((bf16[64,32,512]{2,1,0:T(8,128)(2,1)}), bf16[64,32,512]{2,1,0:T(8,128)(2,1)S(1)}, u32[]{:S(2)}, u32[]{:S(2)}) async-start(bf16[64,32,512]{2,1,0:T(8,128)(2,1)} %broadcast_in_dim.20), calls=%async_computation | async-start | bytes 4194304 | tf_op jit(solution)/shard_map/all_to_all | solution.py:18
  23.2 113.8 %collective-permute-start = (bf16[256]{0:T(256)(128)(2,1)S(1)}, bf16[256]{0:T(256)(128)(2,1)S(1)}, u32[]{:S(2)}, u32[]{:S(2)}) collective-permute-start(bf16[256]{0:T(256)(128)(2,1)S(1)} %get-tuple-element.3), channel_id=1, source_target_pairs={{0,256},{128,384},{1,257},{129,385},{2,258},{130,386},{3,259},{131... | collective-permute-start | bytes 1544 | tf_op jit(solution)/shard_map/ppermute | solution.py:41
  122.6 3.4 %copy-start = (bf16[512,4096]{1,0:T(8,128)(2,1)S(1)}, bf16[512,4096]{1,0:T(8,128)(2,1)}, u32[]{:S(2)}) copy-start(bf16[512,4096]{1,0:T(8,128)(2,1)} %all-gather.2.cloned.1.call-done) | copy-start | bytes 12582916
  126.0 18.5 %copy-start.3 = (f32[1,512]{1,0:T(1,128)S(1)}, f32[1,512]{1,0:T(1,128)}, u32[]{:S(2)}) copy-start(f32[1,512]{1,0:T(1,128)} %param.8) | copy-start | bytes 6148
  131.6 12.8 %all-to-all-start.2 = ((f32[4,512,1]{1,2,0:T(1,128)}), f32[4,512,1]{1,2,0:T(1,128)S(1)}, u32[]{:S(2)}, u32[]{:S(2)}) async-start(f32[4,512,1]{1,2,0:T(1,128)} %broadcast_in_dim.22), calls=%async_computation.2 | async-start | bytes 16384 | tf_op jit(solution)/shard_map/all_to_all | solution.py:18
  137.1 11.8 %collective-permute-start.1 = (bf16[512,256]{0,1:T(8,128)(2,1)S(1)}, bf16[512,256]{0,1:T(8,128)(2,1)S(1)}, u32[]{:S(2)}, u32[]{:S(2)}) collective-permute-start(bf16[512,256]{0,1:T(8,128)(2,1)S(1)} %slice.57), channel_id=1, source_target_pairs={{0,256},{128,384},{1,257},{129,385},{2,258},{130,386},{3,259},{131... | collective-permute-start | bytes 786440 | tf_op jit(solution)/shard_map/ppermute | solution.py:41
Sparse Core Ops, SparseCore 0:
  10.1 112.4 all-gather.1
where the time goes:
time: 245 us; the launch traced here: 241 us
  blocking collectives  86.2 us (35%)
  waiting for transfers between devices  74.9 us (31%)
  starting transfers between devices  35.5 us (14%)
  between operations  16 us (7%)
  matrix products  10.9 us (4%)
  other arithmetic  10.2 us (4%)
  local copies, waits for them, and re-layouts  7.63 us (3%)
    all_to_all x1, blocking collectives, sum_by_axis(): lax.all_to_all(nearer, far, split_axis=0, concat_axis=0, tiled=True)  65.9 us
    all_gather x1, waiting for transfers between devices, shards(): features = lax.all_gather(hidden, 'sec', axis=1, tiled=True)  37.8 us
    all_to_all x2, waiting for transfers between devices, copy_for_each(): return lax.all_to_all(copies, axis, split_axis=0, concat_axis=0, tiled=True)  35.6 us
    all_to_all x2, starting transfers between devices, copy_for_each(): return lax.all_to_all(copies, axis, split_axis=0, concat_axis=0, tiled=True)  18.4 us
    ppermute x2, starting transfers between devices, from_behind(): return lax.ppermute(array, axis, pairs)  17 us
    all_to_all x1, blocking collectives, copy_for_each(): return lax.all_to_all(copies, axis, split_axis=0, concat_axis=0, tiled=True)  10.6 us
    all_to_all x1, blocking collectives, sent_and_summed(): lax.all_to_all(tiles, axis, split_axis=0, concat_axis=0, tiled=True)  9.74 us
    dot_general x1, matrix products, shards(): jnp.dot(normed, whole_slab, preferred_element_type=jnp.float32)  4.91 us
  transfers between devices with their start and end apart: 5, of which 3 were waited for; matrix products, arithmetic and copies ran while one was open for 8% of the time, Pallas kernels for 0%

commit v1 on v0

v1 whole, which is shorter than its diff:
```python
import jax
import jax.numpy as jnp
from jax import lax
from jax.experimental import pallas as pl
from jax.experimental.pallas import tpu as pltpu
from jax.sharding import Mesh
from jax.sharding import PartitionSpec as P

AXES = ("h", "zl", "y", "x", "c")
FSDP = AXES[1:]
MESH = pl.DeviceIdType.MESH

NH, NZ, NY, NX, NC = 4, 2, 8, 4, 2
LEN = 512
SKIP = 64
TOK = (LEN - SKIP) // NH
SEQ = NZ * NC
ROWS = SEQ * TOK
FB = 1024
COLS = 128
D = NH * FB

KL_COEF = 0.1
DISCOUNT = 1.0
TRACE_DECAY = 0.95
NORM_EPS = 1e-05
HIGHEST = lax.Precision.HIGHEST

GROUP = [(a, b, e) for a in range(NH) for b in range(NZ) for e in range(NC) if (a, b, e) != (0, 0, 0)]


class Ids:
    def __init__(self):
        self.used = 0

    def take(self, count):
        first = self.used
        self.used += count
        return first


def plan():
    ids = Ids()
    out = {}
    for name in ("wg", "sd", "mg"):
        out[name] = ids.take(len(GROUP))
    out["hn"], out["hf"], out["hd"] = ids.take(3), ids.take(4), ids.take(8)
    for kind in ("ag", "rs"):
        for part in ("A", "B"):
            for axis, size in (("x", NX), ("y", NY)):
                for way in chains(size):
                    zl, sign, steps = way
                    out[kind, part, axis, zl, sign] = ids.take(steps)
    out["fn"] = ids.take(NH * NC)
    out["local"] = ids.take(2)
    out["total"] = ids.used
    return out


def chains(size):
    far, near = size // 2, size // 2 - 1
    return [(0, 1, far), (1, -1, far), (0, -1, near), (1, 1, near)]


PLAN = plan()


def kernel(
    hid, win, head, refl, spans, grad_out, adv_out,
    X, W, SIDE, MSG, SS, ACC, SL, G, ROWS4, STAGE, LAND, FIN, FR,
    ssem, rsem,
):
    h, zl, y, x, c = (lax.axis_index(a) for a in AXES)
    p = zl * NC + c
    pend = []

    def send(src, dst, sid, dev, rid=None):
        copy = pltpu.make_async_remote_copy(
            src_ref=src,
            dst_ref=dst,
            send_sem=ssem.at[sid],
            recv_sem=rsem.at[sid if rid is None else rid],
            device_id=dev,
            device_id_type=MESH,
        )
        copy.start()
        pend.append(copy)

    def arrived(ref, sid):
        pltpu.make_async_copy(ref, ref, rsem.at[sid]).wait()

    def peer(dh, dz, dc):
        return (lax.rem(h + dh, NH), lax.rem(zl + dz, NZ), y, x, lax.rem(c + dc, NC))

    def origin(dh, dz, dc):
        return (lax.rem(h + NH - dh, NH), lax.rem(zl + NZ - dz, NZ), lax.rem(c + NC - dc, NC))

    def place(axis, by):
        return lax.rem(x + 2 * NX + by, NX) if axis == "x" else lax.rem(y + 2 * NY + by, NY)

    def ring(axis, by):
        if axis == "x":
            return (h, zl, y, place("x", by), c)
        return (h, zl, place("y", by), x, c)

    barrier = pltpu.get_barrier_semaphore()
    mates = [peer(*o) for o in GROUP] + [ring("x", 1), ring("x", -1), ring("y", 1), ring("y", -1)]
    for dev in mates:
        pl.semaphore_signal(barrier, inc=1, device_id=dev, device_id_type=MESH)
    SIDE[h, p, 0:1, :] = refl[...]
    SIDE[h, p, 1:2, :] = jnp.full((1, LEN), spans[0, 0], jnp.int32).astype(jnp.float32)
    SIDE[h, p, 2:3, :] = jnp.full((1, LEN), spans[0, 1], jnp.int32).astype(jnp.float32)
    SIDE[h, p, 3:4, :] = head[...].astype(jnp.float32)
    SIDE[h, p, 4:8, :] = jnp.zeros((4, LEN), jnp.float32)
    MSG[h, p] = jnp.zeros((16, COLS), jnp.float32)
    SS[...] = jnp.zeros_like(SS)
    pl.semaphore_wait(barrier, len(mates))

    def wpiece(hs, zs, cs):
        return W.at[hs, zs * NY + y, x, pl.ds(pl.multiple_of(cs * 32, 32), 32), :]

    def wcols(zs, cs):
        return win.at[0, :, pl.ds(pl.multiple_of((zs * NC + cs) * COLS, COLS), COLS)]

    own_w = pltpu.make_async_copy(wcols(zl, c), wpiece(h, zl, c), rsem.at[PLAN["local"]])
    own_w.start()
    for n, off in enumerate(GROUP):
        dev = peer(*off)
        send(wcols(dev[1], dev[4]), wpiece(h, zl, c), PLAN["wg"] + n, dev)

    def unit(hd):
        return hid.at[pl.ds(pl.multiple_of(SKIP + hd * TOK, 16), TOK), :]

    partner = (h, 1 - zl, y, x, c)
    sibling = (h, zl, y, x, 1 - c)
    up, far, down = (lax.rem(h + by, NH) for by in (1, 2, 3))
    own_x = pltpu.make_async_copy(unit(h), X.at[h, p], rsem.at[PLAN["local"] + 1])
    own_x.start()
    send(unit(far), X.at[h, p], PLAN["hn"] + 2, (far, 1 - zl, y, x, c))
    send(unit(up), X.at[h, p], PLAN["hn"], (up, 0, y, x, c), PLAN["hn"] + zl)
    send(unit(down), X.at[h, p], PLAN["hn"] + 1, (down, 1, y, x, c), PLAN["hn"] + zl)
    send(unit(h), X.at[h, p], PLAN["hf"], partner)
    send(unit(h), X.at[h, p], PLAN["hd"], sibling)
    for n, off in enumerate(GROUP):
        send(SIDE.at[h, p], SIDE.at[h, p], PLAN["sd"] + n, peer(*off))

    def beside(z):
        return lax.rem(h + 3 + 2 * z, NH)

    def roles(z, core):
        first = [(h, z * NC + core), (beside(z), core), (beside(z), NC + core), (far, (1 - z) * NC + core)]
        other = 1 - z
        second = [(h, other * NC + core), (beside(other), core), (beside(other), NC + core), (far, z * NC + core)]
        return first, second

    firsts, seconds = roles(zl, c)
    theirs = sum(roles(zl, 1 - c), [])

    def squares(block, row):
        wide = X[block, row].astype(jnp.float32)
        wide = wide * wide
        part = wide[:, :COLS]
        for k in range(1, FB // COLS):
            part += wide[:, k * COLS : (k + 1) * COLS]
        SS[row] += part

    def first_arrived(n):
        block, row = firsts[n]
        ref = X.at[block, row]
        arrived(ref, PLAN["hn"] + n - 1)
        send(ref, ref, PLAN["hf"] + n, partner)
        send(ref, ref, PLAN["hd"] + n, sibling)
        squares(block, row)

    def second_arrived(n):
        block, row = seconds[n]
        ref = X.at[block, row]
        arrived(ref, PLAN["hf"] + n)
        send(ref, ref, PLAN["hd"] + 4 + n, sibling)
        squares(block, row)

    def third_arrived(n):
        block, row = theirs[n]
        arrived(X.at[block, row], PLAN["hd"] + n)
        squares(block, row)

    def piece(part, axis, half, pos):
        slabs = pl.ds(0 if part == "A" else 2, 2)
        if part == "A":
            if axis == "x":
                return W.at[slabs, half * NY + y, pos]
            return W.at[slabs, half * NY + pos]
        if axis == "y":
            return W.at[slabs, half * NY + pos, x]
        return W.at[slabs, pl.ds(half * NY, NY), pos]

    def gather_start(part, axis):
        for half, sign, _ in chains(NX if axis == "x" else NY):
            own = piece(part, axis, half, place(axis, 0))
            send(own, own, PLAN["ag", part, axis, half, sign], ring(axis, sign))

    def gather_step(part, axis, step):
        for half, sign, steps in chains(NX if axis == "x" else NY):
            if step > steps:
                continue
            base = PLAN["ag", part, axis, half, sign]
            got = piece(part, axis, half, place(axis, -sign * step))
            arrived(got, base + step - 1)
            if step < steps:
                send(got, got, base + step, ring(axis, sign))

    own_w.wait()
    for n, off in enumerate(GROUP):
        arrived(wpiece(*origin(*off)), PLAN["wg"] + n)
    gather_start("A", "x")
    gather_start("B", "y")
    gather_step("A", "x", 1)
    gather_step("B", "y", 1)
    gather_step("A", "x", 2)
    gather_start("A", "y")
    gather_step("B", "y", 2)
    gather_step("B", "y", 3)
    first_arrived(1)
    first_arrived(2)
    gather_step("B", "y", 4)
    gather_start("B", "x")
    gather_step("A", "y", 1)
    first_arrived(3)
    own_x.wait()
    squares(*firsts[0])
    gather_step("A", "y", 2)
    for n in range(3):
        second_arrived(n)
    gather_step("B", "x", 1)
    gather_step("A", "y", 3)
    second_arrived(3)
    for n in range(8):
        third_arrived(n)
    gather_step("B", "x", 2)
    gather_step("A", "y", 4)
    for n, off in enumerate(GROUP):
        hs, zs, cs = origin(*off)
        arrived(SIDE.at[hs, zs * NC + cs], PLAN["sd"] + n)

    ACC[...] = jnp.zeros_like(ACC)

    def project(j, carry):
        tokens = X[j].reshape(ROWS, FB)
        for k in range(2):
            sides = [W[2 * k + e, pl.ds(4 * j, 4)].reshape(FB, COLS) for e in range(2)]
            both = jnp.concatenate(sides, axis=1)
            product = jnp.dot(tokens, both, preferred_element_type=jnp.float32)
            ACC[:, :, 2 * COLS * k : 2 * COLS * (k + 1)] += product.reshape(SEQ, TOK, 2 * COLS)
        return carry

    lax.fori_loop(0, NH, project, 0)

    heads = [SIDE[s, p, 3:4, pl.ds(pl.multiple_of(p * COLS, COLS), COLS)] for s in range(4)]
    ones = jnp.ones((8, COLS), jnp.float32)

    def row_sums(values):
        sums = lax.dot_general(
            ones, values, (((1,), (1,)), ((), ())), precision=HIGHEST, preferred_element_type=jnp.float32
        )
        return sums[0:1, :]

    for i in range(SEQ):
        meansq = jnp.sum(SS[i], axis=1, keepdims=True) * (1.0 / D)
        scale = lax.rsqrt(meansq + NORM_EPS)
        weighted = []
        for s in range(4):
            raw = ACC[i, :, s * COLS : (s + 1) * COLS] * scale
            pre = raw.astype(jnp.bfloat16).astype(jnp.float32)
            sigmoid = 1.0 / (1.0 + jnp.exp(-pre))
            weighted.append(heads[s] * (pre * sigmoid))
            if s < 2:
                slope = sigmoid * (1.0 + pre * (1.0 - sigmoid))
                ACC[i, :, s * COLS : (s + 1) * COLS] = scale * heads[s] * slope
        MSG[h, p, i : i + 1, 0:TOK] = row_sums(weighted[0] + weighted[1])
        MSG[h, p, 4 + i : 5 + i, 0:TOK] = row_sums(weighted[2])
        MSG[h, p, 8 + i : 9 + i, 0:TOK] = row_sums(weighted[3])
    for n, off in enumerate(GROUP):
        send(MSG.at[h, p], MSG.at[h, p], PLAN["mg"] + n, peer(*off))

    for i in range(SEQ):
        for kind in range(3):
            ROWS4[kind, i : i + 1, :] = SIDE[h, i, kind : kind + 1, :]
    for n, off in enumerate(GROUP):
        hs, zs, cs = origin(*off)
        arrived(MSG.at[hs, zs * NC + cs], PLAN["mg"] + n)

    whole = jnp.zeros((16, LEN), jnp.float32)
    for a in range(NH):
        total = (MSG[a, 0] + MSG[a, 1]) + (MSG[a, 2] + MSG[a, 3])
        wide = jnp.concatenate([total, jnp.zeros((16, LEN - COLS), jnp.float32)], axis=1)
        whole += pltpu.roll(wide, SKIP + a * TOK, 1)
    log_prob, value_est, scores = whole[0:4], whole[4:8], whole[8:12]
    position = lax.broadcasted_iota(jnp.int32, (SEQ, LEN), 1)
    ref, starts, ending = ROWS4[0, 0:4, :], ROWS4[1, 0:4, :], ROWS4[2, 0:4, :]
    at = position.astype(jnp.float32)
    inside = jnp.where((at >= starts) & (at < ending), 1.0, 0.0)
    last_tok = jnp.where(at == ending - 1.0, 1.0, 0.0)
    follow = jnp.where(at + 1.0 < ending, 1.0, 0.0)
    reward = -KL_COEF * (log_prob - ref) * inside + scores * last_tok
    next_value = pltpu.roll(value_est, LEN - 1, 1)
    trail = (reward + DISCOUNT * next_value * follow - value_est) * inside
    span = 1
    while span < LEN:
        later = jnp.where(position + span < LEN, pltpu.roll(trail, LEN - span, 1), 0.0)
        trail += (DISCOUNT * TRACE_DECAY) ** span * later
        span *= 2
    advantage = trail * inside
    signal = -advantage / (ending - starts)
    mine = lax.broadcasted_iota(jnp.int32, (SEQ, LEN), 0) == p
    adv_out[...] = jnp.sum(jnp.where(mine, advantage, 0.0), axis=0, keepdims=True)

    near = jnp.zeros((SEQ, COLS), jnp.float32)
    for a in range(NH):
        turned = pltpu.roll(signal, LEN - SKIP - a * TOK, 1)[:, :COLS]
        near += jnp.where(h == a, turned, 0.0)
    square = jnp.concatenate([near, jnp.zeros((COLS - SEQ, COLS), jnp.float32)], axis=0).T
    for i in range(SEQ):
        factor = square[0:TOK, i : i + 1]
        SL[i] = (factor * ACC[i, :, 0 : 2 * COLS]).astype(jnp.bfloat16)

    def share(block, carry):
        j = lax.div(block, 4)
        lanes = pl.ds(pl.multiple_of(lax.rem(block, 4) * 256, 256), 256)
        tokens = X[j, :, :, lanes].reshape(ROWS, 256)
        product = lax.dot_general(
            tokens, SL[...].reshape(ROWS, 2 * COLS), (((0,), (0,)), ((), ())), preferred_element_type=jnp.float32
        )
        G[0, block] = product[:, :COLS].reshape(NX, 64, COLS)
        G[1, block] = product[:, COLS:].reshape(NX, 64, COLS)
        return carry

    lax.fori_loop(0, NZ * NY, share, 0)

    def at_of(part, axis, half, pos):
        if part == "A":
            return (0, half * NY + y, pos) if axis == "x" else (0, half * NY + pos)
        return (1, pl.ds(half * NY, NY), pos) if axis == "x" else (1, half * NY + pos, x)

    def room(buf, part, axis, sid):
        n = sid - PLAN["rs", part, axis, 0, 1]
        return buf[part, axis].at[n]

    def sum_send(part, axis, half, sign, steps, step):
        sid = PLAN["rs", part, axis, half, sign] + step - 1
        own = G[at_of(part, axis, half, place(axis, sign * (steps + 1 - step)))]
        if step > 1:
            own += room(LAND, part, axis, sid - 1)[...].astype(jnp.float32)
        stage = room(STAGE, part, axis, sid)
        stage[...] = own.astype(jnp.bfloat16)
        send(stage, room(LAND, part, axis, sid), sid, ring(axis, sign))

    def sum_step(part, axis, step):
        for half, sign, steps in chains(NX if axis == "x" else NY):
            if step > steps:
                continue
            if step > 0:
                sid = PLAN["rs", part, axis, half, sign] + step - 1
                arrived(room(LAND, part, axis, sid), sid)
                if step == steps:
                    mine_at = at_of(part, axis, half, place(axis, 0))
                    G[mine_at] = G[mine_at] + room(LAND, part, axis, sid)[...].astype(jnp.float32)
            if step < steps:
                sum_send(part, axis, half, sign, steps, step + 1)

    sum_step("A", "y", 0)
    sum_step("B", "x", 0)
    sum_step("A", "y", 1)
    sum_step("B", "x", 1)
    sum_step("A", "y", 2)
    sum_step("B", "x", 2)
    sum_step("B", "y", 0)
    sum_step("A", "y", 3)
    sum_step("B", "y", 1)
    sum_step("A", "y", 4)
    sum_step("A", "x", 0)
    sum_step("B", "y", 2)
    sum_step("A", "x", 1)
    sum_step("B", "y", 3)
    sum_step("A", "x", 2)
    sum_step("B", "y", 4)

    local = []
    for k in range(2):
        for half in range(NZ):
            FIN[k, half] = G[k, half * NY + y, x].astype(jnp.bfloat16)
            for core in range(NC):
                dest_h = k + 2 * zl
                src = FIN.at[k, half, pl.ds(core * 32, 32), :]
                dst = FR.at[h, c]
                rid = PLAN["fn"] + h * NC + c
                sid = PLAN["fn"] + (k * NZ + half) * NC + core
                here = (dest_h == h) & (half == zl) & (core == c)
                remote = pltpu.make_async_remote_copy(
                    src_ref=src,
                    dst_ref=dst,
                    send_sem=ssem.at[sid],
                    recv_sem=rsem.at[rid],
                    device_id=(dest_h, half, y, x, core),
                    device_id_type=MESH,
                )
                keep = pltpu.make_async_copy(src, dst, rsem.at[rid])
                pl.when(here)(keep.start)
                pl.when(jnp.logical_not(here))(remote.start)
                local.append((here, remote))
    for a in range(NH):
        for core in range(NC):
            arrived(FR.at[a, core], PLAN["fn"] + a * NC + core)
    for core in range(NC):
        parts = [FR[a, core].astype(jnp.float32) for a in range(NH)]
        grad_out[0, :, core * COLS : (core + 1) * COLS] = (parts[0] + parts[1]) + (parts[2] + parts[3])
    for here, remote in local:
        pl.when(jnp.logical_not(here))(remote.wait_send)
    for copy in pend:
        copy.wait_send()


def shards(hidden, window_proj, head_weights, ref_logprob, resp_spans):
    vmem = pl.BlockSpec(memory_space=pltpu.VMEM)
    hbm = pl.BlockSpec(memory_space=pl.ANY)
    bf16, f32 = jnp.bfloat16, jnp.float32
    rooms = {
        ("A", "y"): pltpu.VMEM((14, NX, 64, COLS), bf16),
        ("A", "x"): pltpu.VMEM((6, 64, COLS), bf16),
        ("B", "x"): pltpu.VMEM((6, NY, 64, COLS), bf16),
        ("B", "y"): pltpu.VMEM((14, 64, COLS), bf16),
    }
    return pl.pallas_call(
        kernel,
        out_shape=(
            jax.ShapeDtypeStruct((1, 32, 2 * COLS), f32),
            jax.ShapeDtypeStruct((1, LEN), f32),
        ),
        in_specs=[hbm, hbm, vmem, vmem, pl.BlockSpec(memory_space=pltpu.SMEM)],
        out_specs=(vmem, vmem),
        scratch_shapes=[
            pltpu.VMEM((NH, SEQ, TOK, FB), bf16),
            pltpu.VMEM((4, NZ * NY, NX, 64, COLS), bf16),
            pltpu.VMEM((NH, SEQ, 8, LEN), f32),
            pltpu.VMEM((NH, SEQ, 16, COLS), f32),
            pltpu.VMEM((SEQ, TOK, COLS), f32),
            pltpu.VMEM((SEQ, TOK, 4 * COLS), f32),
            pltpu.VMEM((SEQ, TOK, 2 * COLS), bf16),
            pltpu.VMEM((2, NZ * NY, NX, 64, COLS), f32),
            pltpu.VMEM((3, 8, LEN), f32),
            rooms,
            rooms,
            pltpu.VMEM((2, NZ, 64, COLS), bf16),
            pltpu.VMEM((NH, NC, 32, COLS), bf16),
            pltpu.SemaphoreType.DMA((PLAN["total"],)),
            pltpu.SemaphoreType.DMA((PLAN["total"],)),
        ],
        compiler_params=pltpu.CompilerParams(
            collective_id=0, has_side_effects=True, vmem_limit_bytes=48 * 1024 * 1024
        ),
    )(hidden, window_proj, head_weights, ref_logprob, resp_spans)


def solution(mesh):
    finer = Mesh(mesh.devices.reshape(NH, NZ, NY, NX, NC), AXES)
    return jax.shard_map(
        shards,
        mesh=finer,
        in_specs=(P(FSDP, "h"), P("h", FSDP, None), P("h", None), P(FSDP, None), P(FSDP, None)),
        out_specs=(P("h", FSDP, None), P(FSDP, None)),
        check_vma=False,
    )
```

time: 245 us -> 118 us (0.48); the launches traced: 241 us -> 118 us
  Pallas kernels: 0 us -> 112 us
  blocking collectives: 86.2 us -> 0 us
  waiting for transfers between devices: 74.9 us -> 0 us
  starting transfers between devices: 35.5 us -> 0 us
  between operations: 16 us -> 0.65 us
  matrix products: 10.9 us -> 0 us
  other arithmetic: 10.2 us -> 0 us
    pallas_call x0 -> x1, Pallas kernels: none -> 112 us  [shards(): pl.pallas_call(kernel, out_shape=(jax.ShapeDtypeStruct((1, 32, 2 * COLS),...]
    all_to_all x3 -> x0, blocking collectives: 86.2 us -> none  [the longest x1 65.9 us: sum_by_axis(): lax.all_to_all(nearer, far, split_axis=0, concat_axis=0, tiled=True)]
    all_gather x1 -> x0, waiting for transfers between devices: 37.8 us -> none  [shards(): features = lax.all_gather(hidden, 'sec', axis=1, tiled=True)]
    all_to_all x2 -> x0, waiting for transfers between devices: 35.6 us -> none  [copy_for_each(): return lax.all_to_all(copies, axis, split_axis=0, concat_axis=0, tiled=True)]
    all_to_all x2 -> x0, starting transfers between devices: 18.4 us -> none  [copy_for_each(): return lax.all_to_all(copies, axis, split_axis=0, concat_axis=0, tiled=True)]
    ppermute x2 -> x0, starting transfers between devices: 17 us -> none  [from_behind(): return lax.ppermute(array, axis, pairs)]
    dot_general x3 -> x0, matrix products: 10.9 us -> none  [the longest x1 4.91 us: shards(): jnp.dot(normed, whole_slab, preferred_element_type=jnp.float32)]
    reduce_sum x3 -> x0, other arithmetic: 8.36 us -> none  [the longest x1 3.23 us: normalize(): meansq = jnp.mean(widened * widened, axis=1, keepdims=True)]
  transfers between devices with their start and end apart: 5 -> 0, of which waited for: 3 -> 0; matrix products, arithmetic and copies ran while one was open for 8% -> 0% of each run, Pallas kernels for 0% -> 0%
where the time goes in v1:
time: 118 us
  Pallas kernels  112 us (95%)
  local copies, waits for them, and re-layouts  5.19 us (4%)
    pallas_call x1, Pallas kernels, shards(): pl.pallas_call(kernel, out_shape=(jax.ShapeDtypeStruct((1, 32, 2 * COLS),...  112 us
    unnamed x12, local copies, waits for them, and re-layouts  5.19 us

profile of v1, /device:TPU:1, one launch (start us, length us, event | category | flops | bytes accessed | tf_op | source)
XLA Modules:
  0.0 117.6 jit_solution(13798612098657583413)
XLA Ops:
  0.6 0.0 copy-start
  0.6 1.2 %copy-done = bf16[512,1024]{1,0:T(8,128)(2,1)S(1)} copy-done((bf16[512,1024]{1,0:T(8,128)(2,1)S(1)}, bf16[512,1024]{1,0:T(8,128)(2,1)}, u32[]{:S(2)}) %copy-start) | copy-done | bytes 1048600
  1.9 0.0 copy-start.1
  1.9 0.8 copy-done.1
  2.6 0.0 copy-start.2
  2.6 0.7 copy-done.2
  3.3 0.0 copy-start.3
  3.3 0.7 copy-done.3
  4.0 0.0 copy-start.4
  4.0 0.7 copy-done.4
  4.6 111.7 %shard_map.68 = (f32[1,32,256]{2,1,0:T(8,128)S(1)}, f32[1,512]{1,0:T(1,128)S(1)}) custom-call(bf16[512,1024]{1,0:T(8,128)(2,1)S(1)} %copy-done, bf16[1,32,512]{2,1,0:T(8,128)(2,1)S(1)} %copy-done.1, bf16[1,512]{1,0:T(2,128)(2,1)S(1)} %copy-done.2, f32[1,512]{1,0:T(1,128)S(1)} %copy-done.3, s32[1,2]{1,0:T(1,128)S(1)} %copy-done.4), custom_call_target="tpu_custom_call" | custom-call | tf_op jit(solution)/shard_map/pallas_call | solution.py:432
  116.4 0.6 copy.9
  117.0 0.6 copy.10
Async XLA Ops:
  0.6 1.2 %copy-start = (bf16[512,1024]{1,0:T(8,128)(2,1)S(1)}, bf16[512,1024]{1,0:T(8,128)(2,1)}, u32[]{:S(2)}) copy-start(bf16[512,1024]{1,0:T(8,128)(2,1)} %hid.1) | copy-start | bytes 3145732
  1.9 0.8 copy-start.1
  2.6 0.7 copy-start.2
  3.3 0.7 copy-start.3
  4.0 0.7 copy-start.4

commit v2 on v1

v2 whole, which is shorter than its diff:
```python
import jax
import jax.numpy as jnp
from jax import lax
from jax.experimental import pallas as pl
from jax.experimental.pallas import tpu as pltpu
from jax.sharding import Mesh
from jax.sharding import PartitionSpec as P

AXES = ("h", "zl", "y", "x", "c")
FSDP = AXES[1:]
MESH = pl.DeviceIdType.MESH

NH, NZ, NY, NX, NC = 4, 2, 8, 4, 2
LEN = 512
SKIP = 64
TOK = (LEN - SKIP) // NH
CUT = (48, 64)
SEQ = NZ * NC
ROWS = SEQ * TOK
FB = 1024
COLS = 128
D = NH * FB
NCHIP = NH * NZ

KL_COEF = 0.1
DISCOUNT = 1.0
TRACE_DECAY = 0.95
NORM_EPS = 1e-05
HIGHEST = lax.Precision.HIGHEST

GROUP = [(a, b, e) for a in range(NH) for b in range(NZ) for e in range(NC) if (a, b, e) != (0, 0, 0)]


def chains(size):
    far, near = size // 2, size // 2 - 1
    return [(0, 1, far), (1, -1, far), (0, -1, near), (1, 1, near)]


def plan():
    out = {}
    used = 0

    def take(name, count):
        nonlocal used
        out[name] = used
        used += count

    for name in ("wg", "sd", "mg"):
        take(name, len(GROUP))
    for odd in range(2):
        take(("hn", odd), 3)
        take(("hf", odd), 4)
        take(("hd", odd), 8)
    for kind, part, axis in (
        ("ag", "A", "x"),
        ("ag", "A", "y"),
        ("ag", "B", "y"),
        ("ag", "B", "x"),
        ("rs", "A", "y"),
        ("rs", "B", "x"),
    ):
        for half, sign, steps in chains(NX if axis == "x" else NY):
            take((kind, part, axis, half, sign), steps)
    take(("direct", "x"), NZ * (NX - 1))
    take(("direct", "y"), NZ * (NY - 1))
    take("fn", NH * NC)
    take("local", 8)
    out["total"] = used
    return out


PLAN = plan()


def kernel(
    hid, win, head_in, refl_in, spans_in, grad_out, adv_out,
    X, XT, W, SAY, SIDE, MSG, SS, ACC, SL, G, ROWS4, STAGE, LAND, FIN, FR, HEAD, REFL, SPANS,
    ssem, rsem,
):
    h, zl, y, x, c = (lax.axis_index(a) for a in AXES)
    p = zl * NC + c
    pend = []

    def send(src, dst, sid, dev, rid=None):
        copy = pltpu.make_async_remote_copy(
            src_ref=src,
            dst_ref=dst,
            send_sem=ssem.at[sid],
            recv_sem=rsem.at[sid if rid is None else rid],
            device_id=dev,
            device_id_type=MESH,
        )
        copy.start()
        pend.append(copy)

    def arrived(ref, sid):
        pltpu.make_async_copy(ref, ref, rsem.at[sid]).wait()

    def peer(dh, dz, dc):
        return (lax.rem(h + dh, NH), lax.rem(zl + dz, NZ), y, x, lax.rem(c + dc, NC))

    def origin(dh, dz, dc):
        return (lax.rem(h + NH - dh, NH), lax.rem(zl + NZ - dz, NZ), lax.rem(c + NC - dc, NC))

    def place(axis, by):
        return lax.rem(x + 2 * NX + by, NX) if axis == "x" else lax.rem(y + 2 * NY + by, NY)

    def ring(axis, by):
        if axis == "x":
            return (h, zl, y, place("x", by), c)
        return (h, zl, place("y", by), x, c)

    barrier = pltpu.get_barrier_semaphore()
    mates = [peer(*o) for o in GROUP]
    mates += [ring("x", by) for by in range(1, NX)] + [ring("y", by) for by in range(1, NY)]
    for dev in mates:
        pl.semaphore_signal(barrier, inc=1, device_id=dev, device_id_type=MESH)
    local = PLAN["local"]
    fetches = [
        pltpu.make_async_copy(src, dst, rsem.at[local + n])
        for n, (src, dst) in enumerate(((head_in, HEAD), (refl_in, REFL), (spans_in, SPANS)))
    ]
    for fetch in fetches:
        fetch.start()
    MSG[h, p] = jnp.zeros((8, COLS), jnp.float32)
    SS[...] = jnp.zeros_like(SS)
    SL[...] = jnp.zeros_like(SL)
    for fetch in fetches:
        fetch.wait()
    heads_wide = HEAD[...].astype(jnp.float32)
    for target in range(SEQ):
        for k in range(4):
            SAY[target, k : k + 1, :] = REFL[0:1, k * COLS : (k + 1) * COLS]
        for k in range(2):
            SAY[target, 4 + k : 5 + k, :] = jnp.full((1, COLS), SPANS[0, k], jnp.int32).astype(jnp.float32)
        SAY[target, 6:7, :] = heads_wide[:, target * COLS : (target + 1) * COLS]
        SAY[target, 7:8, :] = jnp.zeros((1, COLS), jnp.float32)
    SIDE[h, p] = SAY[p]
    pl.semaphore_wait(barrier, len(mates))

    def wpiece(hs, zs, cs):
        return W.at[hs, zs * NY + y, x, pl.ds(pl.multiple_of(cs * 32, 32), 32), :]

    def wcols(zs, cs):
        return win.at[0, :, pl.ds(pl.multiple_of((zs * NC + cs) * COLS, COLS), COLS)]

    own_w = pltpu.make_async_copy(wcols(zl, c), wpiece(h, zl, c), rsem.at[local + 3])
    own_w.start()
    for n, off in enumerate(GROUP):
        dev = peer(*off)
        send(wcols(dev[1], dev[4]), wpiece(h, zl, c), PLAN["wg"] + n, dev)

    chip = h * NZ + zl
    sibling = (h, zl, y, x, 1 - c)

    def seen(odd):
        turned = lax.rem(chip + NCHIP - odd, NCHIP)
        return lax.div(turned, NZ), lax.rem(turned, NZ)

    def real(odd, pair, side):
        turned = lax.rem(pair * NZ + side + odd, NCHIP)
        return lax.div(turned, NZ), lax.rem(turned, NZ)

    def rows_of(odd):
        return pl.ds(0, CUT[0]) if odd == 0 else pl.ds(CUT[0], CUT[1])

    def unit(odd, pair):
        start = SKIP + pair * TOK + (CUT[0] if odd else 0)
        return hid.at[pl.ds(pl.multiple_of(start, 16), CUT[odd]), :]

    def slot(odd, pair, side, core):
        block, low = real(odd, pair, side)
        return X.at[block, low * NC + core, rows_of(odd)]

    def roles(odd):
        pair, side = seen(odd)
        far = lax.rem(pair + 2, NH)

        def four(s):
            beside = lax.rem(pair + 3 + 2 * s, NH)
            return [(pair, s), (beside, 0), (beside, 1), (far, 1 - s)]

        return four(side), four(1 - side)

    own_x = []
    for odd in range(2):
        pair, side = seen(odd)
        up, far, down = (lax.rem(pair + by, NH) for by in (1, 2, 3))
        mine_at = slot(odd, pair, side, c)
        keep = pltpu.make_async_copy(unit(odd, pair), mine_at, rsem.at[local + 4 + odd])
        keep.start()
        own_x.append(keep)

        def to(dest, dest_side):
            block, low = real(odd, dest, dest_side)
            return (block, low, y, x, c)

        hn = PLAN["hn", odd]
        send(unit(odd, far), mine_at, hn + 2, to(far, 1 - side))
        send(unit(odd, up), mine_at, hn, to(up, 0), hn + side)
        send(unit(odd, down), mine_at, hn + 1, to(down, 1), hn + side)
        send(unit(odd, pair), mine_at, PLAN["hf", odd], to(pair, 1 - side))
        send(unit(odd, pair), mine_at, PLAN["hd", odd], sibling)
    for n, off in enumerate(GROUP):
        dev = peer(*off)
        send(SAY.at[dev[1] * NC + dev[4]], SIDE.at[h, p], PLAN["sd"] + n, dev)

    def firsts_arrived(odd):
        pair, side = seen(odd)
        block, low = real(odd, pair, 1 - side)
        for n in range(1, 4):
            ref = slot(odd, *roles(odd)[0][n], c)
            arrived(ref, PLAN["hn", odd] + n - 1)
            send(ref, ref, PLAN["hf", odd] + n, (block, low, y, x, c))
            send(ref, ref, PLAN["hd", odd] + n, sibling)

    def seconds_arrived(odd):
        for n in range(4):
            ref = slot(odd, *roles(odd)[1][n], c)
            arrived(ref, PLAN["hf", odd] + n)
            send(ref, ref, PLAN["hd", odd] + 4 + n, sibling)

    def settle(odd, which):
        if which == 0:
            own_x[odd].wait()
        for n in range(4):
            source = roles(odd)[which][n]
            arrived(slot(odd, *source, 1 - c), PLAN["hd", odd] + 4 * which + n)
            block, low = real(odd, *source)
            first = 0 if odd == 0 else CUT[0]
            both = X[block, pl.ds(low * NC, NC), first : first + CUT[odd], :]
            wide = both.astype(jnp.float32)
            wide = wide * wide
            part = wide[:, :, :COLS]
            for k in range(1, FB // COLS):
                part += wide[:, :, k * COLS : (k + 1) * COLS]
            SS[pl.ds(low * NC, NC), first : first + CUT[odd], :] += part
            flat = both.reshape(NC * CUT[odd], FB)
            if NC * CUT[odd] < COLS:
                flat = jnp.concatenate([flat, jnp.zeros((COLS - NC * CUT[odd], FB), jnp.bfloat16)], axis=0)
            lanes = pl.ds(pl.multiple_of((odd * NZ + low) * COLS, COLS), COLS)
            XT[block, :, lanes] = flat.T

    def piece(part, axis, half, pos):
        if part == "A":
            slabs = pl.ds(0, 2 - half)
        else:
            slabs = pl.ds(2 - half, 2 + half)
        if part == "A":
            if axis == "x":
                return W.at[slabs, half * NY + y, pos]
            return W.at[slabs, half * NY + pos]
        if axis == "y":
            return W.at[slabs, half * NY + pos, x]
        return W.at[slabs, pl.ds(half * NY, NY), pos]

    def gather_start(part, axis):
        for half, sign, _ in chains(NX if axis == "x" else NY):
            own = piece(part, axis, half, place(axis, 0))
            send(own, own, PLAN["ag", part, axis, half, sign], ring(axis, sign))

    def gather_step(part, axis, step):
        for half, sign, steps in chains(NX if axis == "x" else NY):
            if step > steps:
                continue
            base = PLAN["ag", part, axis, half, sign]
            got = piece(part, axis, half, place(axis, -sign * step))
            arrived(got, base + step - 1)
            if step < steps:
                send(got, got, base + step, ring(axis, sign))

    own_w.wait()
    for n, off in enumerate(GROUP):
        arrived(wpiece(*origin(*off)), PLAN["wg"] + n)
    gather_start("A", "x")
    gather_start("B", "y")
    gather_step("A", "x", 1)
    gather_step("B", "y", 1)
    gather_step("A", "x", 2)
    gather_start("A", "y")
    firsts_arrived(0)
    gather_step("B", "y", 2)
    gather_step("B", "y", 3)
    gather_step("B", "y", 4)
    gather_start("B", "x")
    settle(0, 0)
    seconds_arrived(0)
    gather_step("A", "y", 1)
    firsts_arrived(1)
    settle(0, 1)
    gather_step("A", "y", 2)
    gather_step("B", "x", 1)
    settle(1, 0)
    gather_step("A", "y", 3)
    seconds_arrived(1)
    settle(1, 1)
    gather_step("B", "x", 2)
    gather_step("A", "y", 4)
    for n, off in enumerate(GROUP):
        hs, zs, cs = origin(*off)
        arrived(SIDE.at[hs, zs * NC + cs], PLAN["sd"] + n)

    ACC[...] = jnp.zeros_like(ACC)

    def project(j, carry):
        tokens = X[j].reshape(ROWS, FB)
        for k in range(2):
            sides = [W[2 * k + e, pl.ds(4 * j, 4)].reshape(FB, COLS) for e in range(2)]
            both = jnp.concatenate(sides, axis=1)
            product = jnp.dot(tokens, both, preferred_element_type=jnp.float32)
            ACC[:, :, 2 * COLS * k : 2 * COLS * (k + 1)] += product.reshape(SEQ, TOK, 2 * COLS)
        return carry

    lax.fori_loop(0, NH, project, 0)

    heads = [SIDE[s, p, 6:7, :] for s in range(4)]
    ones = jnp.ones((8, COLS), jnp.float32)

    def row_sums(values):
        sums = lax.dot_general(
            ones, values, (((1,), (1,)), ((), ())), precision=HIGHEST, preferred_element_type=jnp.float32
        )
        return sums[0:1, :]

    lane = lax.broadcasted_iota(jnp.int32, (1, COLS), 1)
    blocks = (h, lax.rem(h + 3 + zl, NH))
    at_lane = (lane + SKIP + TOK * jnp.where(lane < CUT[0], blocks[0], blocks[1])).astype(jnp.float32)[:, :TOK]
    for i in range(SEQ):
        starts, ending = SIDE[h, i, 4:5, 0:TOK], SIDE[h, i, 5:6, 0:TOK]
        inside = jnp.where((at_lane >= starts) & (at_lane < ending), 1.0, 0.0)
        last_tok = jnp.where(at_lane == ending - 1.0, 1.0, 0.0)
        meansq = jnp.sum(SS[i], axis=1, keepdims=True) * (1.0 / D)
        scale = lax.rsqrt(meansq + NORM_EPS)
        weighted = []
        for s in range(4):
            raw = ACC[i, :, s * COLS : (s + 1) * COLS] * scale
            pre = raw.astype(jnp.bfloat16).astype(jnp.float32)
            sigmoid = 1.0 / (1.0 + jnp.exp(-pre))
            weighted.append(heads[s] * (pre * sigmoid))
            if s < 2:
                slope = sigmoid * (1.0 + pre * (1.0 - sigmoid))
                ACC[i, :, s * COLS : (s + 1) * COLS] = scale * heads[s] * slope
        log_prob = row_sums(weighted[0] + weighted[1])
        MSG[h, p, i : i + 1, 0:TOK] = -KL_COEF * log_prob * inside + row_sums(weighted[3]) * last_tok
        MSG[h, p, 4 + i : 5 + i, 0:TOK] = row_sums(weighted[2])
    for n, off in enumerate(GROUP):
        send(MSG.at[h, p], MSG.at[h, p], PLAN["mg"] + n, peer(*off))

    for i in range(SEQ):
        for k in range(4):
            part = slice(k * COLS, (k + 1) * COLS)
            ROWS4[0, i : i + 1, part] = SIDE[h, i, k : k + 1, :]
            ROWS4[1, i : i + 1, part] = SIDE[h, i, 4:5, :]
            ROWS4[2, i : i + 1, part] = SIDE[h, i, 5:6, :]
    for n, off in enumerate(GROUP):
        hs, zs, cs = origin(*off)
        arrived(MSG.at[hs, zs * NC + cs], PLAN["mg"] + n)

    whole = jnp.zeros((8, LEN), jnp.float32)
    for a in range(NH):
        nxt = (a + 1) % NH
        early = jnp.where(lane < CUT[0], MSG[a, 0] + MSG[a, 1], MSG[nxt, 0] + MSG[nxt, 1])
        total = early + (MSG[a, 2] + MSG[a, 3])
        wide = jnp.concatenate([total, jnp.zeros((8, LEN - COLS), jnp.float32)], axis=1)
        whole += pltpu.roll(wide, SKIP + a * TOK, 1)
    gains, value_est = whole[0:4], whole[4:8]
    position = lax.broadcasted_iota(jnp.int32, (SEQ, LEN), 1)
    ref, starts, ending = ROWS4[0, 0:4, :], ROWS4[1, 0:4, :], ROWS4[2, 0:4, :]
    at = position.astype(jnp.float32)
    inside = jnp.where((at >= starts) & (at < ending), 1.0, 0.0)
    follow = jnp.where(at + 1.0 < ending, 1.0, 0.0)
    reward = gains + KL_COEF * ref * inside
    next_value = pltpu.roll(value_est, LEN - 1, 1)
    trail = (reward + DISCOUNT * next_value * follow - value_est) * inside
    span = 1
    while span < LEN:
        later = jnp.where(position + span < LEN, pltpu.roll(trail, LEN - span, 1), 0.0)
        trail += (DISCOUNT * TRACE_DECAY) ** span * later
        span *= 2
    advantage = trail * inside
    signal = -advantage / (ending - starts)
    mine = lax.broadcasted_iota(jnp.int32, (SEQ, LEN), 0) == p
    adv_out[...] = jnp.sum(jnp.where(mine, advantage, 0.0), axis=0, keepdims=True)

    near = jnp.zeros((SEQ, COLS), jnp.float32)
    for a in range(NH):
        turned = pltpu.roll(signal, LEN - SKIP - a * TOK, 1)[:, :COLS]
        wanted = jnp.where(lane < CUT[0], blocks[0], blocks[1]) == a
        near += jnp.where(wanted, turned, 0.0)
    square = jnp.concatenate([near, jnp.zeros((COLS - SEQ, COLS), jnp.float32)], axis=0).T
    for i in range(SEQ):
        factor = square[0:TOK, i : i + 1]
        slopes = (factor * ACC[i, :, 0 : 2 * COLS]).astype(jnp.bfloat16)
        low, core = i // NC, i % NC
        for odd in range(2):
            first = (odd * NZ + low) * COLS + core * CUT[odd]
            taken = slice(0, CUT[0]) if odd == 0 else slice(CUT[0], TOK)
            SL[first : first + CUT[odd], :] = slopes[taken]

    def share(half, pos):
        block = half * NY + lax.rem(pos + 2 * NY, NY)
        j = lax.div(block, 4)
        features = pl.ds(pl.multiple_of(lax.rem(block, 4) * 256, 256), 256)
        product = jnp.dot(XT[j, features, :], SL[...], preferred_element_type=jnp.float32)
        G[0, block] = product[:, :COLS].reshape(NX, 64, COLS)
        G[1, block] = product[:, COLS:].reshape(NX, 64, COLS)

    def at_of(part, axis, half, pos):
        if part == "A":
            return (0, half * NY + y, pos) if axis == "x" else (0, half * NY + pos)
        return (1, pl.ds(half * NY, NY), pos) if axis == "x" else (1, half * NY + pos, x)

    def room(buf, part, axis, sid):
        return buf[part, axis].at[sid - PLAN["rs", part, axis, 0, 1]]

    def sum_send(part, axis, half, sign, steps, step):
        sid = PLAN["rs", part, axis, half, sign] + step - 1
        own = G[at_of(part, axis, half, place(axis, sign * (steps + 1 - step)))]
        if step > 1:
            own += room(LAND, part, axis, sid - 1)[...].astype(jnp.float32)
        stage = room(STAGE, part, axis, sid)
        stage[...] = own.astype(jnp.bfloat16)
        send(stage, room(LAND, part, axis, sid), sid, ring(axis, sign))

    def sum_step(part, axis, step):
        for half, sign, steps in chains(NX if axis == "x" else NY):
            if step > steps:
                continue
            sid = PLAN["rs", part, axis, half, sign] + step - 1
            arrived(room(LAND, part, axis, sid), sid)
            if step == steps:
                mine_at = at_of(part, axis, half, place(axis, 0))
                G[mine_at] = G[mine_at] + room(LAND, part, axis, sid)[...].astype(jnp.float32)
            else:
                sum_send(part, axis, half, sign, steps, step + 1)

    def direct_send(part, axis):
        size = NX if axis == "x" else NY
        for by in sorted(range(1, size), key=lambda d: -min(d, size - d)):
            for half in range(NZ):
                n = half * (size - 1) + by - 1
                stage = STAGE[part, axis].at[n]
                stage[...] = G[at_of(part, axis, half, place(axis, by))].astype(jnp.bfloat16)
                send(stage, LAND[part, axis].at[n], PLAN["direct", axis] + n, ring(axis, by))

    def direct_take(part, axis, k):
        size = NX if axis == "x" else NY
        for half in range(NZ):
            total = G[at_of(part, axis, half, place(axis, 0))]
            for by in range(1, size):
                n = half * (size - 1) + by - 1
                arrived(LAND[part, axis].at[n], PLAN["direct", axis] + n)
                total += LAND[part, axis][n].astype(jnp.float32)
            FIN[k, half] = total.astype(jnp.bfloat16)

    for half, sign, steps in chains(NY):
        share(half, y + sign * steps)
        sum_send("A", "y", half, sign, steps, 1)

    def shares(n, carry):
        share(0, y + 3 - n)
        share(1, y - 3 + n)
        return carry

    lax.fori_loop(0, NY - 2, shares, 0)
    for half, sign, steps in chains(NX):
        sum_send("B", "x", half, sign, steps, 1)
    sum_step("A", "y", 1)
    sum_step("B", "x", 1)
    sum_step("A", "y", 2)
    sum_step("B", "x", 2)
    direct_send("B", "y")
    sum_step("A", "y", 3)
    sum_step("A", "y", 4)
    direct_send("A", "x")

    handed = []
    for k, part, axis in ((1, "B", "y"), (0, "A", "x")):
        direct_take(part, axis, k)
        for half in range(NZ):
            for core in range(NC):
                dest_h = k + 2 * zl
                src = FIN.at[k, half, pl.ds(core * 32, 32), :]
                dst = FR.at[h, c]
                rid = PLAN["fn"] + h * NC + c
                sid = PLAN["fn"] + (k * NZ + half) * NC + core
                here = (dest_h == h) & (half == zl) & (core == c)
                remote = pltpu.make_async_remote_copy(
                    src_ref=src,
                    dst_ref=dst,
                    send_sem=ssem.at[sid],
                    recv_sem=rsem.at[rid],
                    device_id=(dest_h, half, y, x, core),
                    device_id_type=MESH,
                )
                keep = pltpu.make_async_copy(src, dst, rsem.at[rid])
                pl.when(here)(keep.start)
                pl.when(jnp.logical_not(here))(remote.start)
                handed.append((here, remote))
    for a in range(NH):
        for core in range(NC):
            arrived(FR.at[a, core], PLAN["fn"] + a * NC + core)
    for core in range(NC):
        parts = [FR[a, core].astype(jnp.float32) for a in range(NH)]
        grad_out[0, :, core * COLS : (core + 1) * COLS] = (parts[0] + parts[1]) + (parts[2] + parts[3])
    for here, remote in handed:
        pl.when(jnp.logical_not(here))(remote.wait_send)
    for copy in pend:
        copy.wait_send()


def shards(hidden, window_proj, head_weights, ref_logprob, resp_spans):
    vmem = pl.BlockSpec(memory_space=pltpu.VMEM)
    hbm = pl.BlockSpec(memory_space=pl.ANY)
    bf16, f32 = jnp.bfloat16, jnp.float32
    rooms = {
        ("A", "y"): pltpu.VMEM((14, NX, 64, COLS), bf16),
        ("A", "x"): pltpu.VMEM((6, 64, COLS), bf16),
        ("B", "x"): pltpu.VMEM((6, NY, 64, COLS), bf16),
        ("B", "y"): pltpu.VMEM((14, 64, COLS), bf16),
    }
    return pl.pallas_call(
        kernel,
        out_shape=(
            jax.ShapeDtypeStruct((1, 32, 2 * COLS), f32),
            jax.ShapeDtypeStruct((1, LEN), f32),
        ),
        in_specs=[hbm] * 5,
        out_specs=(vmem, vmem),
        scratch_shapes=[
            pltpu.VMEM((NH, SEQ, TOK, FB), bf16),
            pltpu.VMEM((NH, FB, 4 * COLS), bf16),
            pltpu.VMEM((4, NZ * NY, NX, 64, COLS), bf16),
            pltpu.VMEM((SEQ, 8, COLS), f32),
            pltpu.VMEM((NH, SEQ, 8, COLS), f32),
            pltpu.VMEM((NH, SEQ, 8, COLS), f32),
            pltpu.VMEM((SEQ, TOK, COLS), f32),
            pltpu.VMEM((SEQ, TOK, 4 * COLS), f32),
            pltpu.VMEM((4 * COLS, 2 * COLS), bf16),
            pltpu.VMEM((2, NZ * NY, NX, 64, COLS), f32),
            pltpu.VMEM((3, 8, LEN), f32),
            rooms,
            rooms,
            pltpu.VMEM((2, NZ, 64, COLS), bf16),
            pltpu.VMEM((NH, NC, 32, COLS), bf16),
            pltpu.VMEM((1, LEN), bf16),
            pltpu.VMEM((1, LEN), f32),
            pltpu.SMEM((1, 2), jnp.int32),
            pltpu.SemaphoreType.DMA((PLAN["total"],)),
            pltpu.SemaphoreType.DMA((PLAN["total"],)),
        ],
        compiler_params=pltpu.CompilerParams(
            collective_id=0, has_side_effects=True, vmem_limit_bytes=60 * 1024 * 1024
        ),
    )(hidden, window_proj, head_weights, ref_logprob, resp_spans)


def solution(mesh):
    finer = Mesh(mesh.devices.reshape(NH, NZ, NY, NX, NC), AXES)
    return jax.shard_map(
        shards,
        mesh=finer,
        in_specs=(P(FSDP, "h"), P("h", FSDP, None), P("h", None), P(FSDP, None), P(FSDP, None)),
        out_specs=(P("h", FSDP, None), P(FSDP, None)),
        check_vma=False,
    )
```

time: 118 us -> 113 us (0.958)
  local copies, waits for them, and re-layouts: 5.19 us -> 1.96 us
  Pallas kernels: 112 us -> 110 us
    unnamed x12 -> x4, local copies, waits for them, and re-layouts: 5.19 us -> 1.96 us
    pallas_call x1, Pallas kernels: 112 us -> 110 us  [shards(): pl.pallas_call(kernel, out_shape=(jax.ShapeDtypeStruct((1, 32, 2 * COLS),...]
where the time goes in v2:
time: 113 us; the launch traced here: 112 us
  Pallas kernels  110 us (97%)
  local copies, waits for them, and re-layouts  1.96 us (2%)
    pallas_call x1, Pallas kernels, shards(): pl.pallas_call(kernel, out_shape=(jax.ShapeDtypeStruct((1, 32, 2 * COLS),...  110 us

profile of v2, /device:TPU:1, one launch (start us, length us, event | category | flops | bytes accessed | tf_op | source)
XLA Modules:
  0.0 112.3 jit_solution(15119458453409419777)
XLA Ops:
  0.6 109.7 %shard_map.68 = (f32[1,32,256]{2,1,0:T(8,128)}, f32[1,512]{1,0:T(1,128)}) custom-call(bf16[512,1024]{1,0:T(8,128)(2,1)} %hid.1, bf16[1,32,512]{2,1,0:T(8,128)(2,1)} %win.1, bf16[1,512]{1,0:T(2,128)(2,1)} %head_in.1, f32[1,512]{1,0:T(1,128)} %refl_in.1, s32[1,2]{1,0:T(1,128)} %spans_in.1), custom_call_target="tpu_custom_call" | custom-call | tf_op jit(solution)/shard_map/pallas_call | solution.py:522
  110.3 0.0 copy-start
  110.3 1.4 %copy.9 = f32[1,32,256]{2,1,0:T(8,128)} copy(f32[1,32,256]{2,1,0:T(8,128)} %get-tuple-element.4) | data formatting | bytes 65536
  111.7 0.0 copy-done
  111.7 0.6 copy.10
Async XLA Ops:
  110.3 1.4 %copy-start = (f32[1,512]{1,0:T(1,128)S(1)}, f32[1,512]{1,0:T(1,128)}, u32[]{:S(2)}) copy-start(f32[1,512]{1,0:T(1,128)} %get-tuple-element.5) | copy-start | bytes 6148

commit v3 on v2

--- a/solution.py
+++ b/solution.py
@@ -48,19 +48,18 @@
     for name in ("wg", "sd", "mg"):
         take(name, len(GROUP))
     for odd in range(2):
-        take(("hn", odd), 3)
-        take(("hf", odd), 4)
+        for way in (1, -1):
+            take(("hn", odd, way), 8)
         take(("hd", odd), 8)
-    for kind, part, axis in (
-        ("ag", "A", "x"),
-        ("ag", "A", "y"),
-        ("ag", "B", "y"),
-        ("ag", "B", "x"),
-        ("rs", "A", "y"),
-        ("rs", "B", "x"),
-    ):
+    for part, axis in (("A", "x"), ("A", "y"), ("B", "y")):
         for half, sign, steps in chains(NX if axis == "x" else NY):
-            take((kind, part, axis, half, sign), steps)
+            take(("ag", part, axis, half, sign), steps)
+    for half, sign, steps in chains(NX):
+        take(("ag", "B", "x", half, sign), steps * NY)
+    for part, axis in (("A", "y"), ("B", "x")):
+        for sub in range(2):
+            for half, sign, steps in chains(NX if axis == "x" else NY):
+                take(("rs", part, axis, sub, half, sign), steps)
     take(("direct", "x"), NZ * (NX - 1))
     take(("direct", "y"), NZ * (NY - 1))
     take("fn", NH * NC)
@@ -81,7 +80,7 @@
     p = zl * NC + c
     pend = []
 
-    def send(src, dst, sid, dev, rid=None):
+    def send(src, dst, sid, dev, rid=None, when=None):
         copy = pltpu.make_async_remote_copy(
             src_ref=src,
             dst_ref=dst,
@@ -90,11 +89,18 @@
             device_id=dev,
             device_id_type=MESH,
         )
-        copy.start()
-        pend.append(copy)
-
-    def arrived(ref, sid):
-        pltpu.make_async_copy(ref, ref, rsem.at[sid]).wait()
+        if when is None:
+            copy.start()
+        else:
+            pl.when(when)(copy.start)
+        pend.append((when, copy))
+
+    def arrived(ref, sid, when=None):
+        copy = pltpu.make_async_copy(ref, ref, rsem.at[sid])
+        if when is None:
+            copy.wait()
+        else:
+            pl.when(when)(copy.wait)
 
     def peer(dh, dz, dc):
         return (lax.rem(h + dh, NH), lax.rem(zl + dz, NZ), y, x, lax.rem(c + dc, NC))
@@ -122,6 +128,135 @@
     ]
     for fetch in fetches:
         fetch.start()
+    pl.semaphore_wait(barrier, len(mates))
+
+    def wpiece(hs, zs, cs):
+        return W.at[hs, zs * NY + y, x, pl.ds(pl.multiple_of(cs * 32, 32), 32), :]
+
+    def wcols(zs, cs):
+        return win.at[0, :, pl.ds(pl.multiple_of((zs * NC + cs) * COLS, COLS), COLS)]
+
+    own_w = pltpu.make_async_copy(wcols(zl, c), wpiece(h, zl, c), rsem.at[local + 3])
+    own_w.start()
+    for n, off in enumerate(GROUP):
+        dev = peer(*off)
+        send(wcols(dev[1], dev[4]), wpiece(h, zl, c), PLAN["wg"] + n, dev)
+
+    chip = h * NZ + zl
+    sibling = (h, zl, y, x, 1 - c)
+
+    def turn(by):
+        return lax.rem(chip + 2 * NCHIP + by, NCHIP)
+
+    def next_chip(way):
+        to = turn(way)
+        return (lax.div(to, NZ), lax.rem(to, NZ), y, x, c)
+
+    def rows_of(odd):
+        return pl.ds(0, CUT[0]) if odd == 0 else pl.ds(CUT[0], CUT[1])
+
+    def unit(odd, pair):
+        start = SKIP + pair * TOK + (CUT[0] if odd else 0)
+        return hid.at[pl.ds(pl.multiple_of(start, 16), CUT[odd]), :]
+
+    def kept(odd, origin, core):
+        return X.at[origin * NC + core, rows_of(odd)]
+
+    def passing(odd, way, n):
+        return X.at[NCHIP * NC + (0 if way == 1 else 2) + n, rows_of(odd)]
+
+    def side_of(odd, way):
+        side = lax.rem(chip + odd, NZ)
+        return side if way == 1 else 1 - side
+
+    def hid_sem(odd, way, step, high):
+        return PLAN["hn", odd, way] + 2 * (step - 1) + high
+
+    def own_pair(odd):
+        return lax.div(turn(-odd), NZ)
+
+    def far_unit(odd, way, high):
+        side = side_of(odd, way)
+        if way == 1:
+            return unit(odd, lax.div(turn(side + 2 * high - odd), NZ))
+        return unit(odd, lax.div(turn(-1 - side - 2 * high - odd), NZ))
+
+    def hid_send(odd, way, step, high):
+        side = side_of(odd, way)
+        origin = turn(-way * (step - 1))
+        at_next = kept(odd, origin, c)
+        when = None
+        if step == 1:
+            src = far_unit(odd, way, high)
+            dst = passing(odd, way, 0) if high else at_next
+        elif step == 2:
+            src = passing(odd, way, 0) if high else kept(odd, origin, c)
+            dst = at_next
+            if high:
+                dst = X.at[
+                    jnp.where(side == 0, NCHIP * NC + (0 if way == 1 else 2) + 1, origin * NC + c), rows_of(odd)
+                ]
+            else:
+                when = side == 0
+        elif step == 3:
+            src = X.at[jnp.where(side == 1, NCHIP * NC + (0 if way == 1 else 2) + 1, origin * NC + c), rows_of(odd)]
+            dst = at_next
+        else:
+            src, dst, when = kept(odd, origin, c), at_next, side == 0
+        send(src, dst, hid_sem(odd, way, step, high), next_chip(way), when=when)
+
+    def share_unit(odd, n, origin):
+        ref = kept(odd, origin, c)
+        send(ref, ref, PLAN["hd", odd] + n, sibling)
+
+    ORIGINS = (0, -1, 1, -2, 2, -3, 3, 4)
+
+    def hid_take(odd, way, step, high):
+        side = side_of(odd, way)
+        origin = turn(-way * step)
+        sem = hid_sem(odd, way, step, high)
+        n = ORIGINS.index(-way * step) if step < 4 else 7
+        ref = kept(odd, origin, c)
+        if step == 1 and high:
+            arrived(passing(odd, way, 0), sem)
+            hid_send(odd, way, 2, 1)
+        elif step == 1:
+            arrived(ref, sem)
+            hid_send(odd, way, 2, 0)
+            share_unit(odd, n, origin)
+        elif step == 2 and high:
+            arrived(ref, sem)
+            hid_send(odd, way, 3, 1)
+        elif step == 2:
+            arrived(ref, sem, side == 1)
+            share_unit(odd, n, origin)
+        elif step == 3:
+            arrived(ref, sem)
+            hid_send(odd, way, 4, 1)
+            share_unit(odd, n, origin)
+        else:
+            arrived(ref, sem, side == 1)
+
+    def takes(step, high):
+        for odd in (1, 0):
+            for way in (1, -1):
+                hid_take(odd, way, step, high)
+        if step == 4:
+            for odd in (1, 0):
+                share_unit(odd, 7, turn(4))
+
+    own_x = []
+    for odd in range(2):
+        keep = pltpu.make_async_copy(unit(odd, own_pair(odd)), kept(odd, chip, c), rsem.at[local + 4 + odd])
+        keep.start()
+        own_x.append(keep)
+    for high in (1, 0):
+        for odd in (1, 0):
+            for way in (1, -1):
+                hid_send(odd, way, 1, high)
+    for odd in range(2):
+        send(unit(odd, own_pair(odd)), kept(odd, chip, c), PLAN["hd", odd], sibling)
+
     MSG[h, p] = jnp.zeros((8, COLS), jnp.float32)
     SS[...] = jnp.zeros_like(SS)
     SL[...] = jnp.zeros_like(SL)
@@ -136,99 +271,19 @@
         SAY[target, 6:7, :] = heads_wide[:, target * COLS : (target + 1) * COLS]
         SAY[target, 7:8, :] = jnp.zeros((1, COLS), jnp.float32)
     SIDE[h, p] = SAY[p]
-    pl.semaphore_wait(barrier, len(mates))
-
-    def wpiece(hs, zs, cs):
-        return W.at[hs, zs * NY + y, x, pl.ds(pl.multiple_of(cs * 32, 32), 32), :]
-
-    def wcols(zs, cs):
-        return win.at[0, :, pl.ds(pl.multiple_of((zs * NC + cs) * COLS, COLS), COLS)]
-
-    own_w = pltpu.make_async_copy(wcols(zl, c), wpiece(h, zl, c), rsem.at[local + 3])
-    own_w.start()
-    for n, off in enumerate(GROUP):
-        dev = peer(*off)
-        send(wcols(dev[1], dev[4]), wpiece(h, zl, c), PLAN["wg"] + n, dev)
-
-    chip = h * NZ + zl
-    sibling = (h, zl, y, x, 1 - c)
-
-    def seen(odd):
-        turned = lax.rem(chip + NCHIP - odd, NCHIP)
-        return lax.div(turned, NZ), lax.rem(turned, NZ)
-
-    def real(odd, pair, side):
-        turned = lax.rem(pair * NZ + side + odd, NCHIP)
-        return lax.div(turned, NZ), lax.rem(turned, NZ)
-
-    def rows_of(odd):
-        return pl.ds(0, CUT[0]) if odd == 0 else pl.ds(CUT[0], CUT[1])
-
-    def unit(odd, pair):
-        start = SKIP + pair * TOK + (CUT[0] if odd else 0)
-        return hid.at[pl.ds(pl.multiple_of(start, 16), CUT[odd]), :]
-
-    def slot(odd, pair, side, core):
-        block, low = real(odd, pair, side)
-        return X.at[block, low * NC + core, rows_of(odd)]
-
-    def roles(odd):
-        pair, side = seen(odd)
-        far = lax.rem(pair + 2, NH)
-
-        def four(s):
-            beside = lax.rem(pair + 3 + 2 * s, NH)
-            return [(pair, s), (beside, 0), (beside, 1), (far, 1 - s)]
-
-        return four(side), four(1 - side)
-
-    own_x = []
-    for odd in range(2):
-        pair, side = seen(odd)
-        up, far, down = (lax.rem(pair + by, NH) for by in (1, 2, 3))
-        mine_at = slot(odd, pair, side, c)
-        keep = pltpu.make_async_copy(unit(odd, pair), mine_at, rsem.at[local + 4 + odd])
-        keep.start()
-        own_x.append(keep)
-
-        def to(dest, dest_side):
-            block, low = real(odd, dest, dest_side)
-            return (block, low, y, x, c)
-
-        hn = PLAN["hn", odd]
-        send(unit(odd, far), mine_at, hn + 2, to(far, 1 - side))
-        send(unit(odd, up), mine_at, hn, to(up, 0), hn + side)
-        send(unit(odd, down), mine_at, hn + 1, to(down, 1), hn + side)
-        send(unit(odd, pair), mine_at, PLAN["hf", odd], to(pair, 1 - side))
-        send(unit(odd, pair), mine_at, PLAN["hd", odd], sibling)
     for n, off in enumerate(GROUP):
         dev = peer(*off)
         send(SAY.at[dev[1] * NC + dev[4]], SIDE.at[h, p], PLAN["sd"] + n, dev)
 
-    def firsts_arrived(odd):
-        pair, side = seen(odd)
-        block, low = real(odd, pair, 1 - side)
-        for n in range(1, 4):
-            ref = slot(odd, *roles(odd)[0][n], c)
-            arrived(ref, PLAN["hn", odd] + n - 1)
-            send(ref, ref, PLAN["hf", odd] + n, (block, low, y, x, c))
-            send(ref, ref, PLAN["hd", odd] + n, sibling)
-
-    def seconds_arrived(odd):
-        for n in range(4):
-            ref = slot(odd, *roles(odd)[1][n], c)
-            arrived(ref, PLAN["hf", odd] + n)
-            send(ref, ref, PLAN["hd", odd] + 4 + n, sibling)
-
     def settle(odd, which):
-        if which == 0:
-            own_x[odd].wait()
-        for n in range(4):
-            source = roles(odd)[which][n]
-            arrived(slot(odd, *source, 1 - c), PLAN["hd", odd] + 4 * which + n)
-            block, low = real(odd, *source)
+        for n in which:
+            if n == 0:
+                own_x[odd].wait()
+            origin = turn(ORIGINS[n])
+            block, low = lax.div(origin, NZ), lax.rem(origin, NZ)
+            arrived(kept(odd, origin, 1 - c), PLAN["hd", odd] + n)
             first = 0 if odd == 0 else CUT[0]
-            both = X[block, pl.ds(low * NC, NC), first : first + CUT[odd], :]
+            both = X[pl.ds(origin * NC, NC), first : first + CUT[odd], :]
             wide = both.astype(jnp.float32)
             wide = wide * wide
             part = wide[:, :, :COLS]
@@ -268,34 +323,74 @@
             arrived(got, base + step - 1)
             if step < steps:
                 send(got, got, base + step, ring(axis, sign))
+            if part == "B":
+                across_start(half, (-sign * step) % NY)
+
+    def cell(half, by, pos):
+        return W.at[pl.ds(2 - half, 2 + half), half * NY + place("y", by), pos]
+
+    def across_start(half, by):
+        for other, sign, steps in chains(NX):
+            if other == half:
+                own = cell(half, by, x)
+                send(own, own, PLAN["ag", "B", "x", half, sign] + by * steps, ring("x", sign))
+
+    def across_step(by, step):
+        for half, sign, steps in chains(NX):
+            if step > steps:
+                continue
+            base = PLAN["ag", "B", "x", half, sign] + by * steps
+            got = cell(half, by, place("x", -sign * step))
+            arrived(got, base + step - 1)
+            if step < steps:
+                send(got, got, base + step, ring("x", sign))
 
     own_w.wait()
     for n, off in enumerate(GROUP):
         arrived(wpiece(*origin(*off)), PLAN["wg"] + n)
     gather_start("A", "x")
     gather_start("B", "y")
+    for half in range(NZ):
+        across_start(half, 0)
+    takes(1, 1)
     gather_step("A", "x", 1)
     gather_step("B", "y", 1)
     gather_step("A", "x", 2)
     gather_start("A", "y")
-    firsts_arrived(0)
+    across_step(0, 1)
     gather_step("B", "y", 2)
+    takes(1, 0)
+    across_step(1, 1)
+    across_step(7, 1)
     gather_step("B", "y", 3)
+    takes(2, 1)
+    across_step(0, 2)
+    across_step(2, 1)
+    across_step(6, 1)
     gather_step("B", "y", 4)
-    gather_start("B", "x")
-    settle(0, 0)
-    seconds_arrived(0)
     gather_step("A", "y", 1)
-    firsts_arrived(1)
-    settle(0, 1)
+    takes(2, 0)
+    for odd in range(2):
+        settle(odd, (0, 1, 2))
+    across_step(1, 2)
+    across_step(7, 2)
+    across_step(3, 1)
+    across_step(5, 1)
     gather_step("A", "y", 2)
-    gather_step("B", "x", 1)
-    settle(1, 0)
+    takes(3, 1)
+    across_step(2, 2)
+    across_step(6, 2)
+    across_step(4, 1)
+    for odd in range(2):
+        settle(odd, (3, 4))
     gather_step("A", "y", 3)
-    seconds_arrived(1)
-    settle(1, 1)
-    gather_step("B", "x", 2)
+    across_step(3, 2)
+    across_step(5, 2)
+    takes(4, 1)
+    across_step(4, 2)
     gather_step("A", "y", 4)
+    for odd in range(2):
+        settle(odd, (5, 6, 7))
     for n, off in enumerate(GROUP):
         hs, zs, cs = origin(*off)
         arrived(SIDE.at[hs, zs * NC + cs], PLAN["sd"] + n)
@@ -303,7 +398,7 @@
     ACC[...] = jnp.zeros_like(ACC)
 
     def project(j, carry):
-        tokens = X[j].reshape(ROWS, FB)
+        tokens = X[pl.ds(4 * j, 4)].reshape(ROWS, FB)
         for k in range(2):
             sides = [W[2 * k + e, pl.ds(4 * j, 4)].reshape(FB, COLS) for e in range(2)]
             both = jnp.concatenate(sides, axis=1)
@@ -405,34 +500,38 @@
         G[0, block] = product[:, :COLS].reshape(NX, 64, COLS)
         G[1, block] = product[:, COLS:].reshape(NX, 64, COLS)
 
-    def at_of(part, axis, half, pos):
+    def at_of(part, axis, half, pos, sub=None):
         if part == "A":
-            return (0, half * NY + y, pos) if axis == "x" else (0, half * NY + pos)
-        return (1, pl.ds(half * NY, NY), pos) if axis == "x" else (1, half * NY + pos, x)
+            if axis == "x":
+                return (0, half * NY + y, pos)
+            return (0, half * NY + pos, pl.ds(2 * sub, 2))
+        if axis == "x":
+            return (1, pl.ds(half * NY + 4 * sub, 4), pos)
+        return (1, half * NY + pos, x)
 
     def room(buf, part, axis, sid):
-        return buf[part, axis].at[sid - PLAN["rs", part, axis, 0, 1]]
-
-    def sum_send(part, axis, half, sign, steps, step):
-        sid = PLAN["rs", part, axis, half, sign] + step - 1
-        own = G[at_of(part, axis, half, place(axis, sign * (steps + 1 - step)))]
+        return buf[part, axis].at[sid - PLAN["rs", part, axis, 0, 0, 1]]
+
+    def sum_send(part, axis, sub, half, sign, steps, step):
+        sid = PLAN["rs", part, axis, sub, half, sign] + step - 1
+        own = G[at_of(part, axis, half, place(axis, sign * (steps + 1 - step)), sub)]
         if step > 1:
             own += room(LAND, part, axis, sid - 1)[...].astype(jnp.float32)
         stage = room(STAGE, part, axis, sid)
         stage[...] = own.astype(jnp.bfloat16)
         send(stage, room(LAND, part, axis, sid), sid, ring(axis, sign))
 
-    def sum_step(part, axis, step):
+    def sum_step(part, axis, step, sub):
         for half, sign, steps in chains(NX if axis == "x" else NY):
             if step > steps:
                 continue
-            sid = PLAN["rs", part, axis, half, sign] + step - 1
+            sid = PLAN["rs", part, axis, sub, half, sign] + step - 1
             arrived(room(LAND, part, axis, sid), sid)
             if step == steps:
-                mine_at = at_of(part, axis, half, place(axis, 0))
+                mine_at = at_of(part, axis, half, place(axis, 0), sub)
                 G[mine_at] = G[mine_at] + room(LAND, part, axis, sid)[...].astype(jnp.float32)
             else:
-                sum_send(part, axis, half, sign, steps, step + 1)
+                sum_send(part, axis, sub, half, sign, steps, step + 1)
 
     def direct_send(part, axis):
         size = NX if axis == "x" else NY
@@ -455,7 +554,9 @@
 
     for half, sign, steps in chains(NY):
         share(half, y + sign * steps)
-        sum_send("A", "y", half, sign, steps, 1)
+        sum_send("A", "y", 0, half, sign, steps, 1)
+    for half, sign, steps in chains(NY):
+        sum_send("A", "y", 1, half, sign, steps, 1)
 
     def shares(n, carry):
         share(0, y + 3 - n)
@@ -463,15 +564,22 @@
         return carry
 
     lax.fori_loop(0, NY - 2, shares, 0)
-    for half, sign, steps in chains(NX):
-        sum_send("B", "x", half, sign, steps, 1)
-    sum_step("A", "y", 1)
-    sum_step("B", "x", 1)
-    sum_step("A", "y", 2)
-    sum_step("B", "x", 2)
+    for sub in range(2):
+        for half, sign, steps in chains(NX):
+            sum_send("B", "x", sub, half, sign, steps, 1)
+    sum_step("A", "y", 1, 0)
+    sum_step("A", "y", 1, 1)
+    sum_step("B", "x", 1, 0)
+    sum_step("B", "x", 1, 1)
+    sum_step("A", "y", 2, 0)
+    sum_step("A", "y", 2, 1)
+    sum_step("B", "x", 2, 0)
+    sum_step("B", "x", 2, 1)
     direct_send("B", "y")
-    sum_step("A", "y", 3)
-    sum_step("A", "y", 4)
+    sum_step("A", "y", 3, 0)
+    sum_step("A", "y", 3, 1)
+    sum_step("A", "y", 4, 0)
+    sum_step("A", "y", 4, 1)
     direct_send("A", "x")
 
     handed = []
@@ -505,8 +613,11 @@
         grad_out[0, :, core * COLS : (core + 1) * COLS] = (parts[0] + parts[1]) + (parts[2] + parts[3])
     for here, remote in handed:
         pl.when(jnp.logical_not(here))(remote.wait_send)
-    for copy in pend:
-        copy.wait_send()
+    for when, copy in pend:
+        if when is None:
+            copy.wait_send()
+        else:
+            pl.when(when)(copy.wait_send)
 
 
 def shards(hidden, window_proj, head_weights, ref_logprob, resp_spans):
@@ -514,9 +625,9 @@
     hbm = pl.BlockSpec(memory_space=pl.ANY)
     bf16, f32 = jnp.bfloat16, jnp.float32
     rooms = {
-        ("A", "y"): pltpu.VMEM((14, NX, 64, COLS), bf16),
+        ("A", "y"): pltpu.VMEM((28, NX // 2, 64, COLS), bf16),
         ("A", "x"): pltpu.VMEM((6, 64, COLS), bf16),
-        ("B", "x"): pltpu.VMEM((6, NY, 64, COLS), bf16),
+        ("B", "x"): pltpu.VMEM((12, NY // 2, 64, COLS), bf16),
         ("B", "y"): pltpu.VMEM((14, 64, COLS), bf16),
     }
     return pl.pallas_call(
@@ -528,7 +639,7 @@
         in_specs=[hbm] * 5,
         out_specs=(vmem, vmem),
         scratch_shapes=[
-            pltpu.VMEM((NH, SEQ, TOK, FB), bf16),
+            pltpu.VMEM((NCHIP * NC + 4, TOK, FB), bf16),
             pltpu.VMEM((NH, FB, 4 * COLS), bf16),
             pltpu.VMEM((4, NZ * NY, NX, 64, COLS), bf16),
             pltpu.VMEM((SEQ, 8, COLS), f32),

time: 113 us -> 104 us (0.920)
  Pallas kernels: 110 us -> 101 us
    pallas_call x1, Pallas kernels: 110 us -> 101 us  [shards(): pl.pallas_call(kernel, out_shape=(jax.ShapeDtypeStruct((1, 32, 2 * COLS),...]
where the time goes in v3:
time: 104 us
  Pallas kernels  101 us (97%)
  local copies, waits for them, and re-layouts  1.96 us (2%)
    pallas_call x1, Pallas kernels, shards(): pl.pallas_call(kernel, out_shape=(jax.ShapeDtypeStruct((1, 32, 2 * COLS),...  101 us

profile of v3, /device:TPU:1, one launch (start us, length us, event | category | flops | bytes accessed | tf_op | source)
XLA Modules:
  0.0 104.1 jit_solution(9013957292856272423)
XLA Ops:
  0.6 101.5 %shard_map.68 = (f32[1,32,256]{2,1,0:T(8,128)}, f32[1,512]{1,0:T(1,128)}) custom-call(bf16[512,1024]{1,0:T(8,128)(2,1)} %hid.1, bf16[1,32,512]{2,1,0:T(8,128)(2,1)} %win.1, bf16[1,512]{1,0:T(2,128)(2,1)} %head_in.1, f32[1,512]{1,0:T(1,128)} %refl_in.1, s32[1,2]{1,0:T(1,128)} %spans_in.1), custom_call_target="tpu_custom_call" | custom-call | tf_op jit(solution)/shard_map/pallas_call | solution.py:633
  102.1 0.0 copy-start
  102.1 1.4 %copy.9 = f32[1,32,256]{2,1,0:T(8,128)} copy(f32[1,32,256]{2,1,0:T(8,128)} %get-tuple-element.4) | data formatting | bytes 65536
  103.5 0.0 copy-done
  103.5 0.6 copy.10
Async XLA Ops:
  102.1 1.4 %copy-start = (f32[1,512]{1,0:T(1,128)S(1)}, f32[1,512]{1,0:T(1,128)}, u32[]{:S(2)}) copy-start(f32[1,512]{1,0:T(1,128)} %get-tuple-element.5) | copy-start | bytes 6148

commit v4 on v3

--- a/solution.py
+++ b/solution.py
@@ -28,7 +28,7 @@
 NORM_EPS = 1e-05
 HIGHEST = lax.Precision.HIGHEST
 
-GROUP = [(a, b, e) for a in range(NH) for b in range(NZ) for e in range(NC) if (a, b, e) != (0, 0, 0)]
+GROUP = [(a, b, e) for a in (2, 1, 3, 0) for b in range(NZ) for e in range(NC) if (a, b, e) != (0, 0, 0)]
 
 
 def chains(size):
@@ -521,9 +521,9 @@
         stage[...] = own.astype(jnp.bfloat16)
         send(stage, room(LAND, part, axis, sid), sid, ring(axis, sign))
 
-    def sum_step(part, axis, step, sub):
+    def sum_step(part, axis, step, sub, only=None):
         for half, sign, steps in chains(NX if axis == "x" else NY):
-            if step > steps:
+            if step > steps or (only is not None and steps != only):
                 continue
             sid = PLAN["rs", part, axis, sub, half, sign] + step - 1
             arrived(room(LAND, part, axis, sid), sid)
@@ -564,22 +564,26 @@
         return carry
 
     lax.fori_loop(0, NY - 2, shares, 0)
+    for long in (2, 1):
+        for sub in range(2):
+            for half, sign, steps in chains(NX):
+                if steps == long:
+                    sum_send("B", "x", sub, half, sign, steps, 1)
     for sub in range(2):
-        for half, sign, steps in chains(NX):
-            sum_send("B", "x", sub, half, sign, steps, 1)
-    sum_step("A", "y", 1, 0)
-    sum_step("A", "y", 1, 1)
-    sum_step("B", "x", 1, 0)
-    sum_step("B", "x", 1, 1)
-    sum_step("A", "y", 2, 0)
-    sum_step("A", "y", 2, 1)
-    sum_step("B", "x", 2, 0)
-    sum_step("B", "x", 2, 1)
+        sum_step("A", "y", 1, sub)
+    for sub in range(2):
+        sum_step("B", "x", 1, sub, only=2)
+    for sub in range(2):
+        sum_step("A", "y", 2, sub)
+    for sub in range(2):
+        sum_step("A", "y", 3, sub)
+    for sub in range(2):
+        sum_step("B", "x", 1, sub, only=1)
+    for sub in range(2):
+        sum_step("B", "x", 2, sub)
     direct_send("B", "y")
-    sum_step("A", "y", 3, 0)
-    sum_step("A", "y", 3, 1)
-    sum_step("A", "y", 4, 0)
-    sum_step("A", "y", 4, 1)
+    for sub in range(2):
+        sum_step("A", "y", 4, sub)
     direct_send("A", "x")
 
     handed = []

time: 104 us -> 99.5 us (0.957)
  Pallas kernels: 101 us -> 96.6 us
    pallas_call x1, Pallas kernels: 101 us -> 96.6 us  [shards(): pl.pallas_call(kernel, out_shape=(jax.ShapeDtypeStruct((1, 32, 2 * COLS),...]
where the time goes in v4:
time: 99.5 us; the launch traced here: 99.3 us
  Pallas kernels  96.6 us (97%)
  local copies, waits for them, and re-layouts  1.96 us (2%)
    pallas_call x1, Pallas kernels, shards(): pl.pallas_call(kernel, out_shape=(jax.ShapeDtypeStruct((1, 32, 2 * COLS),...  96.6 us

profile of v4, /device:TPU:1, one launch (start us, length us, event | category | flops | bytes accessed | tf_op | source)
XLA Modules:
  0.0 99.3 jit_solution(2467259287960810652)
XLA Ops:
  0.6 96.6 %shard_map.68 = (f32[1,32,256]{2,1,0:T(8,128)}, f32[1,512]{1,0:T(1,128)}) custom-call(bf16[512,1024]{1,0:T(8,128)(2,1)} %hid.1, bf16[1,32,512]{2,1,0:T(8,128)(2,1)} %win.1, bf16[1,512]{1,0:T(2,128)(2,1)} %head_in.1, f32[1,512]{1,0:T(1,128)} %refl_in.1, s32[1,2]{1,0:T(1,128)} %spans_in.1), custom_call_target="tpu_custom_call" | custom-call | tf_op jit(solution)/shard_map/pallas_call | solution.py:637
  97.3 0.0 copy-start
  97.3 1.4 %copy.9 = f32[1,32,256]{2,1,0:T(8,128)} copy(f32[1,32,256]{2,1,0:T(8,128)} %get-tuple-element.4) | data formatting | bytes 65536
  98.7 0.0 copy-done
  98.7 0.6 copy.10
Async XLA Ops:
  97.3 1.4 %copy-start = (f32[1,512]{1,0:T(1,128)S(1)}, f32[1,512]{1,0:T(1,128)}, u32[]{:S(2)}) copy-start(f32[1,512]{1,0:T(1,128)} %get-tuple-element.5) | copy-start | bytes 6148

commit v5 on v4

--- a/solution.py
+++ b/solution.py
@@ -51,9 +51,12 @@
         for way in (1, -1):
             take(("hn", odd, way), 8)
         take(("hd", odd), 8)
-    for part, axis in (("A", "x"), ("A", "y"), ("B", "y")):
+    for part, axis in (("A", "x"), ("B", "y")):
         for half, sign, steps in chains(NX if axis == "x" else NY):
             take(("ag", part, axis, half, sign), steps)
+    for sub in range(2):
+        for half, sign, steps in chains(NY):
+            take(("ag", "A", "y", sub, half, sign), steps)
     for half, sign, steps in chains(NX):
         take(("ag", "B", "x", half, sign), steps * NY)
     for part, axis in (("A", "y"), ("B", "x")):
@@ -326,6 +329,25 @@
             if part == "B":
                 across_start(half, (-sign * step) % NY)
 
+    def along(half, by, sub):
+        return W.at[pl.ds(0, 2 - half), half * NY + place("y", by), pl.ds(2 * sub, 2)]
+
+    def along_start(sub):
+        for half, sign, _ in chains(NY):
+            own = along(half, 0, sub)
+            send(own, own, PLAN["ag", "A", "y", sub, half, sign], ring("y", sign))
+
+    def along_step(step):
+        for sub in range(2):
+            for half, sign, steps in chains(NY):
+                if step > steps:
+                    continue
+                base = PLAN["ag", "A", "y", sub, half, sign]
+                got = along(half, -sign * step, sub)
+                arrived(got, base + step - 1)
+                if step < steps:
+                    send(got, got, base + step, ring("y", sign))
+
     def cell(half, by, pos):
         return W.at[pl.ds(2 - half, 2 + half), half * NY + place("y", by), pos]
 
@@ -356,41 +378,36 @@
     gather_step("A", "x", 1)
     gather_step("B", "y", 1)
     gather_step("A", "x", 2)
-    gather_start("A", "y")
+    for sub in range(2):
+        along_start(sub)
     across_step(0, 1)
     gather_step("B", "y", 2)
+    gather_step("B", "y", 3)
     takes(1, 0)
     across_step(1, 1)
     across_step(7, 1)
-    gather_step("B", "y", 3)
+    gather_step("B", "y", 4)
     takes(2, 1)
-    across_step(0, 2)
+    along_step(1)
     across_step(2, 1)
     across_step(6, 1)
-    gather_step("B", "y", 4)
-    gather_step("A", "y", 1)
     takes(2, 0)
-    for odd in range(2):
-        settle(odd, (0, 1, 2))
-    across_step(1, 2)
-    across_step(7, 2)
+    along_step(2)
     across_step(3, 1)
     across_step(5, 1)
-    gather_step("A", "y", 2)
     takes(3, 1)
-    across_step(2, 2)
-    across_step(6, 2)
     across_step(4, 1)
+    along_step(3)
+    takes(4, 1)
     for odd in range(2):
-        settle(odd, (3, 4))
-    gather_step("A", "y", 3)
-    across_step(3, 2)
-    across_step(5, 2)
-    takes(4, 1)
-    across_step(4, 2)
-    gather_step("A", "y", 4)
+        settle(odd, (0, 1, 2,))
     for odd in range(2):
-        settle(odd, (5, 6, 7))
+        settle(odd, (3, 4,))
+    for odd in range(2):
+        settle(odd, (5, 6, 7,))
+    for by in range(NY):
+        across_step(by, 2)
+    along_step(4)
     for n, off in enumerate(GROUP):
         hs, zs, cs = origin(*off)
         arrived(SIDE.at[hs, zs * NC + cs], PLAN["sd"] + n)

time: 99.5 us -> 97.7 us (0.982)
  Pallas kernels: 96.6 us -> 94.9 us
    pallas_call x1, Pallas kernels: 96.6 us -> 94.9 us  [shards(): pl.pallas_call(kernel, out_shape=(jax.ShapeDtypeStruct((1, 32, 2 * COLS),...]
where the time goes in v5:
time: 97.7 us; the launch traced here: 97.5 us
  Pallas kernels  94.9 us (97%)
  local copies, waits for them, and re-layouts  1.96 us (2%)
    pallas_call x1, Pallas kernels, shards(): pl.pallas_call(kernel, out_shape=(jax.ShapeDtypeStruct((1, 32, 2 * COLS),...  94.9 us
    unnamed x4, local copies, waits for them, and re-layouts  1.96 us

profile of v5, /device:TPU:1, one launch (start us, length us, event | category | flops | bytes accessed | tf_op | source)
XLA Modules:
  0.0 97.5 jit_solution(6180921934592665972)
XLA Ops:
  0.6 94.9 %shard_map.68 = (f32[1,32,256]{2,1,0:T(8,128)}, f32[1,512]{1,0:T(1,128)}) custom-call(bf16[512,1024]{1,0:T(8,128)(2,1)} %hid.1, bf16[1,32,512]{2,1,0:T(8,128)(2,1)} %win.1, bf16[1,512]{1,0:T(2,128)(2,1)} %head_in.1, f32[1,512]{1,0:T(1,128)} %refl_in.1, s32[1,2]{1,0:T(1,128)} %spans_in.1), custom_call_target="tpu_custom_call" | custom-call | tf_op jit(solution)/shard_map/pallas_call | solution.py:654
  95.5 0.0 copy-start
  95.5 1.4 %copy.9 = f32[1,32,256]{2,1,0:T(8,128)} copy(f32[1,32,256]{2,1,0:T(8,128)} %get-tuple-element.4) | data formatting | bytes 65536
  96.9 0.0 copy-done
  96.9 0.6 copy.10
Async XLA Ops:
  95.5 1.4 %copy-start = (f32[1,512]{1,0:T(1,128)S(1)}, f32[1,512]{1,0:T(1,128)}, u32[]{:S(2)}) copy-start(f32[1,512]{1,0:T(1,128)} %get-tuple-element.5) | copy-start | bytes 6148

commit v6 on v5

--- a/solution.py
+++ b/solution.py
@@ -262,6 +262,7 @@
 
     MSG[h, p] = jnp.zeros((8, COLS), jnp.float32)
     SS[...] = jnp.zeros_like(SS)
+    ACC[...] = jnp.zeros_like(ACC)
     SL[...] = jnp.zeros_like(SL)
     for fetch in fetches:
         fetch.wait()
@@ -405,25 +406,25 @@
         settle(odd, (3, 4,))
     for odd in range(2):
         settle(odd, (5, 6, 7,))
+    along_step(4)
+
+    def project(j, k):
+        tokens = X[pl.ds(4 * j, 4)].reshape(ROWS, FB)
+        sides = [W[2 * k + e, pl.ds(4 * j, 4)].reshape(FB, COLS) for e in range(2)]
+        both = jnp.concatenate(sides, axis=1)
+        product = jnp.dot(tokens, both, preferred_element_type=jnp.float32)
+        ACC[:, :, 2 * COLS * k : 2 * COLS * (k + 1)] += product.reshape(SEQ, TOK, 2 * COLS)
+        return 0
+
+    lax.fori_loop(0, NH // 2, lambda j, carry: project(j, 0), 0)
     for by in range(NY):
         across_step(by, 2)
-    along_step(4)
     for n, off in enumerate(GROUP):
         hs, zs, cs = origin(*off)
         arrived(SIDE.at[hs, zs * NC + cs], PLAN["sd"] + n)
 
-    ACC[...] = jnp.zeros_like(ACC)
-
-    def project(j, carry):
-        tokens = X[pl.ds(4 * j, 4)].reshape(ROWS, FB)
-        for k in range(2):
-            sides = [W[2 * k + e, pl.ds(4 * j, 4)].reshape(FB, COLS) for e in range(2)]
-            both = jnp.concatenate(sides, axis=1)
-            product = jnp.dot(tokens, both, preferred_element_type=jnp.float32)
-            ACC[:, :, 2 * COLS * k : 2 * COLS * (k + 1)] += product.reshape(SEQ, TOK, 2 * COLS)
-        return carry
-
-    lax.fori_loop(0, NH, project, 0)
+    lax.fori_loop(NH // 2, NH, lambda j, carry: project(j, 0), 0)
+    lax.fori_loop(0, NH, lambda j, carry: project(j, 1), 0)
 
     heads = [SIDE[s, p, 6:7, :] for s in range(4)]
     ones = jnp.ones((8, COLS), jnp.float32)

time: 97.7 us -> 98.3 us (level)
  no operation moved by 1% of the time
where the time goes in v6:
time: 98.3 us; the launch traced here: 98.1 us
  Pallas kernels  95.5 us (97%)
  local copies, waits for them, and re-layouts  1.96 us (2%)
    pallas_call x1, Pallas kernels, shards(): pl.pallas_call(kernel, out_shape=(jax.ShapeDtypeStruct((1, 32, 2 * COLS),...  95.5 us

profile of v6, /device:TPU:1, one launch (start us, length us, event | category | flops | bytes accessed | tf_op | source)
XLA Modules:
  0.0 98.1 jit_solution(2684178940842055155)
XLA Ops:
  0.6 95.5 %shard_map.68 = (f32[1,32,256]{2,1,0:T(8,128)}, f32[1,512]{1,0:T(1,128)}) custom-call(bf16[512,1024]{1,0:T(8,128)(2,1)} %hid.1, bf16[1,32,512]{2,1,0:T(8,128)(2,1)} %win.1, bf16[1,512]{1,0:T(2,128)(2,1)} %head_in.1, f32[1,512]{1,0:T(1,128)} %refl_in.1, s32[1,2]{1,0:T(1,128)} %spans_in.1), custom_call_target="tpu_custom_call" | custom-call | tf_op jit(solution)/shard_map/pallas_call | solution.py:655
  96.2 0.0 copy-start
  96.2 1.4 %copy.9 = f32[1,32,256]{2,1,0:T(8,128)} copy(f32[1,32,256]{2,1,0:T(8,128)} %get-tuple-element.4) | data formatting | bytes 65536
  97.5 0.0 copy-done
  97.6 0.6 copy.10
Async XLA Ops:
  96.2 1.4 %copy-start = (f32[1,512]{1,0:T(1,128)S(1)}, f32[1,512]{1,0:T(1,128)}, u32[]{:S(2)}) copy-start(f32[1,512]{1,0:T(1,128)} %get-tuple-element.5) | copy-start | bytes 6148
